TPU v7x, 256 devices: a whole 4x4x8 slice. The times are simulated.
256 devices in a mesh: row: 128 (over z, x_hi, y, core), band: 2 (over x_lo).
Axes of the slice: x: 4 (x_hi: 2, x_lo: 2; x = x_hi * 2 + x_lo), y: 4, z: 8, core: 2. Of those that a mesh axis runs over, the one named last changes fastest.
Arguments:
- intens: bfloat16 [512, 1024, 768], P('row', None, 'band'), may hold values from -6 to 6
- block_list: int32 [1024, 4], P(None, 'band'), may hold values from 0 to 2, as said below
- block_count: int32 [1024, 2], P(None, 'band'), may hold values from 0 to 2
- pixel_gradient: float32 [2, 768], P(None, 'band'), may hold values from -40 to 40
Outputs:
- image: float32 [2, 512, 1024], P('band', 'row')
Inputs may be any that keep to these rules, and one draw needn't show every extreme that they name: `block_list`: the 2 entries of one scan x-frequency and band differ; entries past the count are valid block numbers and carry no weight.
All inputs are finite; a program needn't handle non-finite values.
Results may differ from a plain program's by a relative error of at most 0.0048.
Values may be sent and summed in bfloat16 or wider, within the bound.
No kernel may reach another device: no remote copies, remote signals or barrier semaphores. Data moves between devices by JAX's collectives and lax.ppermute only.
A program may use at most 128 MiB of HBM per device.

v0:
```python
from functools import partial
import math

import jax
import jax.numpy as jnp
from jax import lax
from jax.sharding import PartitionSpec as P

NX = 1024
PIX_BLK = 128
BLK_BAND = 3
CAP = 2


def factor_pair(rows_index, cols_index, length):
    turns = rows_index[:, None] * cols_index[None, :] % length
    angle = turns.astype(jnp.float32) * (2.0 * math.pi / length)
    norm_factor = 1.0 / math.sqrt(length)
    return (jnp.cos(angle) * norm_factor, jnp.sin(angle) * norm_factor)


def signed_freq(index_values, length):
    return (
        jnp.where(index_values < length // 2, index_values, index_values - length).astype(
            jnp.float32
        )
        / length
    )


def rotation_table(cosine_part, sine_part):
    upper_half = jnp.concatenate([cosine_part, sine_part], axis=1)
    lower_half = jnp.concatenate([-sine_part, cosine_part], axis=1)
    return jnp.concatenate([upper_half, lower_half], axis=0)


def block_freq(source_row, slot_pos, qx_dev):
    return source_row * qx_dev + slot_pos


def component_tables(freq_rows, every_x, band_index):
    cosine_x, sine_x = factor_pair(freq_rows, every_x, NX)
    first_table = jnp.where(band_index == 0, cosine_x, sine_x)
    second_table = jnp.where(band_index == 0, -sine_x, cosine_x)
    return jnp.stack([first_table, second_table], axis=0)


def pick_blocks(values, lists):
    pieces = []
    for slot_pos in range(lists.shape[1]):
        chosen = jnp.zeros(values.shape[:-1] + (PIX_BLK,), values.dtype)
        for block_id in range(BLK_BAND):
            matched = (lists[:, slot_pos] == block_id)[None, :, None, None]
            chosen = jnp.where(
                matched, values[..., block_id * PIX_BLK : (block_id + 1) * PIX_BLK], chosen
            )
        pieces.append(chosen)
    return jnp.concatenate(pieces, axis=-1)


def body(intens, block_list, block_count, pixel_gradient):
    rows_dev = intens.shape[0]
    row_count = lax.axis_size("row")
    qx_dev = NX // row_count
    width_y = rows_dev * row_count
    own_row = lax.axis_index("row")
    band_index = lax.axis_index("band")
    every_x = jnp.arange(NX, dtype=jnp.int32)
    every_y = jnp.arange(width_y, dtype=jnp.int32)
    slots_own = jnp.arange(qx_dev, dtype=jnp.int32)
    freq_of = partial(block_freq, qx_dev=qx_dev)
    owned_freq = freq_of(own_row, slots_own)
    cosine_x, sine_x = factor_pair(every_x, every_x, NX)
    table_x = jnp.concatenate([cosine_x, -sine_x], axis=0).astype(jnp.bfloat16)
    spectrum = jnp.einsum("fx,rxp->frp", table_x, intens, preferred_element_type=jnp.float32)
    spectrum = spectrum.astype(jnp.bfloat16).reshape(2, NX, rows_dev, BLK_BAND * PIX_BLK)
    lists_own = block_list[owned_freq]
    counts_own = block_count[owned_freq, 0]
    picked = pick_blocks(spectrum, block_list)
    received = lax.all_to_all(picked, "row", split_axis=1, concat_axis=2, tiled=True)
    cosine_y, sine_y = factor_pair(every_y, every_y, width_y)
    exact_y = rotation_table(cosine_y, sine_y)
    table_y = exact_y.astype(jnp.bfloat16)
    freq_x = signed_freq(owned_freq, NX)
    freq_y = signed_freq(every_y, width_y)
    gradient = pixel_gradient.reshape(2, BLK_BAND, PIX_BLK)
    slot_index = jnp.arange(CAP, dtype=jnp.int32)
    psi_scale = 1.0 / math.sqrt(lax.axis_size("band") * CAP * PIX_BLK)
    slot_width = CAP * PIX_BLK

    def trotter(freq_slot):

        def compute_live(unused):
            pieces = lax.dynamic_index_in_dim(received, freq_slot, 1, keepdims=False).reshape(
                2 * width_y, slot_width
            )
            along_y = jnp.dot(table_y, pieces, preferred_element_type=jnp.float32)
            real_part = along_y[:width_y]
            imag_part = along_y[width_y:]
            block_ids = lists_own[freq_slot]
            gradient_x = gradient[0][block_ids].reshape(slot_width)
            gradient_y = gradient[1][block_ids].reshape(slot_width)
            live_mask = (slot_index < counts_own[freq_slot]).astype(jnp.float32)
            weight = jnp.broadcast_to(live_mask[:, None], (CAP, PIX_BLK)).reshape(slot_width)
            freq_now = freq_x[freq_slot]
            phase_angle = (
                gradient_x[None, :] * freq_now + gradient_y[None, :] * freq_y[:, None]
            ) * (2.0 * math.pi)
            cosine_t = jnp.cos(phase_angle)
            sine_t = jnp.sin(phase_angle)
            psi_real = jnp.sum(
                (real_part * cosine_t + imag_part * sine_t) * weight[None, :], axis=1
            )
            psi_imag = jnp.sum(
                (imag_part * cosine_t - real_part * sine_t) * weight[None, :], axis=1
            )
            return jnp.stack([psi_real, psi_imag]) * psi_scale

        def give_zeros(unused):
            return jnp.zeros((2, width_y), jnp.float32)

        return lax.cond(counts_own[freq_slot] > 0, compute_live, give_zeros, 0)

    partial_psi = lax.map(trotter, slots_own)
    psi = lax.psum(partial_psi, "band")
    columns = jnp.dot(
        psi.reshape(qx_dev, 2 * width_y),
        exact_y,
        precision=lax.Precision.HIGHEST,
        preferred_element_type=jnp.float32,
    )
    columns = columns.reshape(qx_dev, 2, width_y)
    gathered = lax.all_to_all(columns, "row", split_axis=2, concat_axis=0, tiled=True)
    freq_rows = freq_of(every_x // qx_dev, every_x % qx_dev)
    image = jnp.einsum(
        "qcy,cqx->yx",
        gathered,
        component_tables(freq_rows, every_x, band_index),
        precision=lax.Precision.HIGHEST,
        preferred_element_type=jnp.float32,
    )
    return image[None]


def solution(mesh):
    return jax.shard_map(
        body,
        mesh=mesh,
        in_specs=(P("row", None, "band"), P(None, "band"), P(None, "band"), P(None, "band")),
        out_specs=P("band", "row", None),
        check_vma=False,
    )
```

profile of v0, /device:TPU:2, one launch (start us, length us, event | category | flops | bytes accessed | tf_op | source)
XLA Modules:
  0.0 337.9 jit_solution(4063376921239098651)
XLA Ops:
  0.0 17.1 %negate_convert_fusion = (bf16[1024,1024]{1,0:T(8,128)(2,1)S(1)}, bf16[1024,1024]{1,0:T(8,128)(2,1)S(1)}) fusion(), kind=kLoop, calls=%fused_computation.57 | loop fusion | flops 19922944 | bytes 4194304 | tf_op jit(solution)/shard_map/convert.2
  17.3 7.3 %convolution_convert_fusion = bf16[2048,4,384]{2,0,1:T(8,128)(2,1)S(1)} fusion(bf16[4,1024,384]{2,1,0:T(8,128)(2,1)S(1)} %copy-done, bf16[1024,1024]{1,0:T(8,128)(2,1)S(1)} %get-tuple-element.178, bf16[1024,1024]{1,0:T(8,128)(2,1)S(1)} %get-tuple-element.179), kind=kOutput, calls=%fused_computation.40 | convolution fusion | flops 6453985280 | bytes 13631488 | tf_op jit(solution)/shard_map/fx,rxp->frp/dot_general | solution.py:75
  24.6 1.7 fusion.56
  26.3 22.0 %broadcast_select_fusion.3 = (bf16[2,1024,4,128]{3,0,2,1:T(2,128)(2,1)S(1)}, bf16[2,1024,4,128]{3,0,2,1:T(2,128)(2,1)}) fusion(pred[1024]{0:T(1024)(128)(4,1)S(1)} %get-tuple-element.147, pred[1024]{0:T(1024)(128)(4,1)S(1)} %get-tuple-element.144, pred[1024]{0:T(1024)(128)(4,1)S(1)} %get-tuple-element.143, ...), kind=kLoop, calls=%fused_computation.64 | loop fusion | flops 6291456 | bytes 10491904 | tf_op jit(solution)/shard_map/jit(_where)/select_n | solution.py:54
  48.3 8.0 %pad_maximum_fusion = bf16[2,1024,4,256]{3,0,2,1:T(2,128)(2,1)} fusion(bf16[2,1024,4,128]{3,0,2,1:T(2,128)(2,1)} %get-tuple-element.172, bf16[2,1024,4,128]{3,0,2,1:T(2,128)(2,1)S(1)} %get-tuple-element.171), kind=kLoop, calls=%fused_computation.50 | loop fusion | flops 8388608 | bytes 8388608 | tf_op jit(solution)/shard_map/concatenate | solution.py:58
  56.3 15.7 %all-to-all-start = ((bf16[2,1024,4,256]{3,0,2,1:T(2,128)(2,1)}), bf16[2,1024,4,256]{3,0,2,1:T(2,128)(2,1)}, u32[]{:S(2)}, u32[]{:S(2)}) async-start(bf16[2,1024,4,256]{3,0,2,1:T(2,128)(2,1)} %pad_maximum_fusion), calls=%async_computation | async-start | bytes 8388608 | tf_op jit(solution)/shard_map/all_to_all | solution.py:80
  72.1 1.0 copy.18
  73.1 3.9 %fusion.41 = f32[512,512]{1,0:T(8,128)S(1)} fusion(), kind=kLoop, calls=%fused_computation.84 | loop fusion | flops 4194304 | bytes 1048576 | tf_op jit(solution)/shard_map/neg | solution.py:33
  77.0 4.2 %sine_multiply_fusion.1 = (f32[512,512]{1,0:T(8,128)S(1)}, f32[512,512]{1,0:T(8,128)S(1)}) fusion(), kind=kLoop, calls=%fused_computation.79 | loop fusion | flops 4194304 | bytes 2097152 | tf_op jit(solution)/shard_map/mul | solution.py:19
  81.1 1.0 copy-done.3
  82.2 2.4 fusion.30
  84.6 5.4 %copy.19 = f32[1024,1024]{1,0:T(8,128)} copy(f32[1024,1024]{0,1:T(8,128)} %fusion.30) | data formatting | bytes 8388608 | tf_op jit(solution)/shard_map/dot_general | solution.py:126
  89.9 1.6 gather_fusion.3
  92.2 2.2 fusion.31
  94.4 74.9 %all-to-all-done = bf16[2,1024,4,256]{3,0,2,1:T(2,128)(2,1)} async-done(((bf16[2,1024,4,256]{3,0,2,1:T(2,128)(2,1)}), bf16[2,1024,4,256]{3,0,2,1:T(2,128)(2,1)}, u32[]{:S(2)}, u32[]{:S(2)}) %all-to-all-start) | async-done | bytes 4194336 | tf_op jit(solution)/shard_map/all_to_all | solution.py:80
  169.3 6.2 %copy.17 = bf16[2,8,128,4,256]{4,3,2,1,0:T(4,128)(2,1)} copy(bf16[2,8,128,4,256]{4,0,3,1,2:T(2,128)(2,1)} %bitcast.17) | data formatting | bytes 8388608 | tf_op jit(solution)/shard_map/all_to_all | solution.py:80
  175.5 6.9 %all_to_all.29 = bf16[2,8,512,256]{3,2,1,0:T(8,128)(2,1)} reshape(bf16[2,8,128,4,256]{4,3,2,1,0:T(4,128)(2,1)} %copy.17) | data formatting | bytes 8388608 | tf_op jit(solution)/shard_map/all_to_all | solution.py:80
  182.4 106.4 %while.11 = (s32[]{:T(128)}, f32[8,2,512]{2,1,0:T(2,128)S(1)}, s32[8]{0:T(128)S(1)}, s32[8]{0:T(128)S(1)}, bf16[2,8,512,256]{3,2,1,0:T(8,128)(2,1)}, /*index=5*/...) while((s32[]{:T(128)}, f32[8,2,512]{2,1,0:T(2,128)S(1)}, ...), condition=%wide.region_5.6_spmd.clone, body=%wide.region_0.5_spmd.clone.sunk | while | flops 538579776 | bytes 5816847 | solution.py:124
  186.0 9.7 %conditional.3 = (f32[1,2,512]{2,1,0:T(2,128)S(1)}) conditional(s32[]{:T(128)} %bitcast.72, () %tuple.51, (s32[]{:T(128)}, bf16[2,8,512,256]{3,2,1,0:T(8,128)(2,1)}, bf16[1024,1024]{1,0:T(8,128)(2,1)S(1)}, f32[2,3,128]{2,1,0:T(4,128)S(1)}, s32[8,2]{1,0:T(8,128)S(1)}, /*index=5*/f32[8]{0:T(128)S(1)}, f32[512]{0:T(512)S(1)}, s32[8]{0:T(128)S(1)}, ...), branch_computations={%region_1.1_spmd, %region_2.4_spmd.clone} | conditional | flops 538577664 | bytes 5806290 | solution.py:122
  191.3 1.1 constant_dynamic-slice_fusion
  193.2 2.5 multiply_reduce_fusion.1
  199.3 9.7 %conditional.3 = (f32[1,2,512]{2,1,0:T(2,128)S(1)}) conditional(s32[]{:T(128)} %bitcast.72, () %tuple.51, (s32[]{:T(128)}, bf16[2,8,512,256]{3,2,1,0:T(8,128)(2,1)}, bf16[1024,1024]{1,0:T(8,128)(2,1)S(1)}, f32[2,3,128]{2,1,0:T(4,128)S(1)}, s32[8,2]{1,0:T(8,128)S(1)}, /*index=5*/f32[8]{0:T(128)S(1)}, f32[512]{0:T(512)S(1)}, s32[8]{0:T(128)S(1)}, ...), branch_computations={%region_1.1_spmd, %region_2.4_spmd.clone} | conditional | flops 538577664 | bytes 5806290 | solution.py:122
  204.6 1.1 constant_dynamic-slice_fusion
  206.5 2.5 multiply_reduce_fusion.1
  212.5 9.7 %conditional.3 = (f32[1,2,512]{2,1,0:T(2,128)S(1)}) conditional(s32[]{:T(128)} %bitcast.72, () %tuple.51, (s32[]{:T(128)}, bf16[2,8,512,256]{3,2,1,0:T(8,128)(2,1)}, bf16[1024,1024]{1,0:T(8,128)(2,1)S(1)}, f32[2,3,128]{2,1,0:T(4,128)S(1)}, s32[8,2]{1,0:T(8,128)S(1)}, /*index=5*/f32[8]{0:T(128)S(1)}, f32[512]{0:T(512)S(1)}, s32[8]{0:T(128)S(1)}, ...), branch_computations={%region_1.1_spmd, %region_2.4_spmd.clone} | conditional | flops 538577664 | bytes 5806290 | solution.py:122
  217.9 1.1 constant_dynamic-slice_fusion
  219.8 2.5 multiply_reduce_fusion.1
  225.8 9.7 %conditional.3 = (f32[1,2,512]{2,1,0:T(2,128)S(1)}) conditional(s32[]{:T(128)} %bitcast.72, () %tuple.51, (s32[]{:T(128)}, bf16[2,8,512,256]{3,2,1,0:T(8,128)(2,1)}, bf16[1024,1024]{1,0:T(8,128)(2,1)S(1)}, f32[2,3,128]{2,1,0:T(4,128)S(1)}, s32[8,2]{1,0:T(8,128)S(1)}, /*index=5*/f32[8]{0:T(128)S(1)}, f32[512]{0:T(512)S(1)}, s32[8]{0:T(128)S(1)}, ...), branch_computations={%region_1.1_spmd, %region_2.4_spmd.clone} | conditional | flops 538577664 | bytes 5806290 | solution.py:122
  231.2 1.1 constant_dynamic-slice_fusion
  233.1 2.5 multiply_reduce_fusion.1
  239.1 9.7 %conditional.3 = (f32[1,2,512]{2,1,0:T(2,128)S(1)}) conditional(s32[]{:T(128)} %bitcast.72, () %tuple.51, (s32[]{:T(128)}, bf16[2,8,512,256]{3,2,1,0:T(8,128)(2,1)}, bf16[1024,1024]{1,0:T(8,128)(2,1)S(1)}, f32[2,3,128]{2,1,0:T(4,128)S(1)}, s32[8,2]{1,0:T(8,128)S(1)}, /*index=5*/f32[8]{0:T(128)S(1)}, f32[512]{0:T(512)S(1)}, s32[8]{0:T(128)S(1)}, ...), branch_computations={%region_1.1_spmd, %region_2.4_spmd.clone} | conditional | flops 538577664 | bytes 5806290 | solution.py:122
  244.5 1.1 constant_dynamic-slice_fusion
  246.4 2.5 multiply_reduce_fusion.1
  252.4 9.7 %conditional.3 = (f32[1,2,512]{2,1,0:T(2,128)S(1)}) conditional(s32[]{:T(128)} %bitcast.72, () %tuple.51, (s32[]{:T(128)}, bf16[2,8,512,256]{3,2,1,0:T(8,128)(2,1)}, bf16[1024,1024]{1,0:T(8,128)(2,1)S(1)}, f32[2,3,128]{2,1,0:T(4,128)S(1)}, s32[8,2]{1,0:T(8,128)S(1)}, /*index=5*/f32[8]{0:T(128)S(1)}, f32[512]{0:T(512)S(1)}, s32[8]{0:T(128)S(1)}, ...), branch_computations={%region_1.1_spmd, %region_2.4_spmd.clone} | conditional | flops 538577664 | bytes 5806290 | solution.py:122
  257.8 1.1 constant_dynamic-slice_fusion
  259.7 2.5 multiply_reduce_fusion.1
  265.7 9.7 %conditional.3 = (f32[1,2,512]{2,1,0:T(2,128)S(1)}) conditional(s32[]{:T(128)} %bitcast.72, () %tuple.51, (s32[]{:T(128)}, bf16[2,8,512,256]{3,2,1,0:T(8,128)(2,1)}, bf16[1024,1024]{1,0:T(8,128)(2,1)S(1)}, f32[2,3,128]{2,1,0:T(4,128)S(1)}, s32[8,2]{1,0:T(8,128)S(1)}, /*index=5*/f32[8]{0:T(128)S(1)}, f32[512]{0:T(512)S(1)}, s32[8]{0:T(128)S(1)}, ...), branch_computations={%region_1.1_spmd, %region_2.4_spmd.clone} | conditional | flops 538577664 | bytes 5806290 | solution.py:122
  271.1 1.1 constant_dynamic-slice_fusion
  273.0 2.5 multiply_reduce_fusion.1
  279.0 9.7 %conditional.3 = (f32[1,2,512]{2,1,0:T(2,128)S(1)}) conditional(s32[]{:T(128)} %bitcast.72, () %tuple.51, (s32[]{:T(128)}, bf16[2,8,512,256]{3,2,1,0:T(8,128)(2,1)}, bf16[1024,1024]{1,0:T(8,128)(2,1)S(1)}, f32[2,3,128]{2,1,0:T(4,128)S(1)}, s32[8,2]{1,0:T(8,128)S(1)}, /*index=5*/f32[8]{0:T(128)S(1)}, f32[512]{0:T(512)S(1)}, s32[8]{0:T(128)S(1)}, ...), branch_computations={%region_1.1_spmd, %region_2.4_spmd.clone} | conditional | flops 538577664 | bytes 5806290 | solution.py:122
  284.4 1.1 constant_dynamic-slice_fusion
  286.3 2.5 multiply_reduce_fusion.1
  288.8 8.3 %psum.7 = f32[8,1024]{1,0:T(8,128)S(1)} all-reduce(f32[8,1024]{1,0:T(8,128)S(1)} %bitcast.79), channel_id=1, replica_groups=mesh['row'=128,'band'=2] {'band'}, use_global_device_ids=true, to_apply=%region_6.7 | all-reduce | flops 8192 | bytes 65536 | tf_op jit(solution)/shard_map/psum | solution.py:125
  297.1 5.6 %fusion.42 = f32[8,2,512]{2,0,1:T(8,128)S(1)} fusion(f32[2,512,1024]{2,1,0:T(8,128)} %bitcast.74, f32[8,1024]{1,0:T(8,128)S(1)} %psum.7), kind=kOutput, calls=%fused_computation.85 | convolution fusion | flops 100663296 | bytes 4259840 | tf_op jit(solution)/shard_map/dot_general | solution.py:126
  302.8 1.1 copy.20
  303.8 6.6 %all-to-all-start.1 = ((f32[8,2,512]{0,1,2:T(2,128)}), f32[8,2,512]{0,1,2:T(2,128)S(1)}, u32[]{:S(2)}, u32[]{:S(2)}) async-start(f32[8,2,512]{0,1,2:T(2,128)} %copy.20), calls=%async_computation.1 | async-start | bytes 1048576 | tf_op jit(solution)/shard_map/all_to_all | solution.py:133
  310.4 19.5 %fusion.29 = (f32[1,1024,1024]{2,1,0:T(8,128)}, f32[1,1024,1024]{2,1,0:T(8,128)}) fusion(s32[1024]{0:T(1024)S(1)} %fusion.51, pred[]{:T(512)S(6)} %eq.83), kind=kLoop, calls=%fused_computation.69 | loop fusion | flops 19922944 | bytes 8392705 | tf_op jit(solution)/shard_map/jit(_where)/select_n | solution.py:43
  330.8 7.1 %fusion.32 = f32[1,4,1024]{2,1,0:T(4,128)} fusion(f32[1024,2,4]{0,2,1:T(4,128)S(1)} %all_to_all.33, f32[1,1024,1024]{2,1,0:T(8,128)} %get-tuple-element.177, f32[1,1024,1024]{2,1,0:T(8,128)} %get-tuple-element.176), kind=kOutput, calls=%fused_computation.75 | convolution fusion | flops 102760448 | bytes 8437760 | tf_op jit(solution)/shard_map/qcy,cqx->yx/dot_general | solution.py:135
  (179 shorter events, 46.1 us)
Async XLA Ops:
  0.0 17.3 %copy-start = (bf16[4,1024,384]{2,1,0:T(8,128)(2,1)S(1)}, bf16[4,1024,384]{2,1,0:T(8,128)(2,1)}, u32[]{:S(2)}) copy-start(bf16[4,1024,384]{2,1,0:T(8,128)(2,1)} %param.8) | copy-start | bytes 9437188
  0.0 17.2 %copy-start.5 = (s32[1024,2]{0,1:T(2,128)S(1)}, s32[1024,2]{0,1:T(2,128)}, u32[]{:S(2)}) copy-start(s32[1024,2]{0,1:T(2,128)} %param.9) | copy-start | bytes 24580
  56.3 16.8 %copy-start.6 = (f32[2,384]{1,0:T(2,128)S(1)}, f32[2,384]{1,0:T(2,128)}, u32[]{:S(2)}) copy-start(f32[2,384]{1,0:T(2,128)} %param.11) | copy-start | bytes 9220
  56.3 113.0 %all-to-all-start = ((bf16[2,1024,4,256]{3,0,2,1:T(2,128)(2,1)}), bf16[2,1024,4,256]{3,0,2,1:T(2,128)(2,1)}, u32[]{:S(2)}, u32[]{:S(2)}) async-start(bf16[2,1024,4,256]{3,0,2,1:T(2,128)(2,1)} %pad_maximum_fusion), calls=%async_computation | async-start | bytes 8388608 | tf_op jit(solution)/shard_map/all_to_all | solution.py:80
  81.1 1.0 copy-start.3
  81.1 8.8 %copy-start.4 = (f32[512,512]{1,0:T(8,128)}, f32[512,512]{1,0:T(8,128)S(1)}, u32[]{:S(2)}) copy-start(f32[512,512]{1,0:T(8,128)S(1)} %get-tuple-element.181) | copy-start | bytes 3145732
  84.6 7.0 %copy-start.2 = (s32[1024,1]{0,1:T(1,128)S(1)}, s32[1024,1]{0,1:T(1,128)}, u32[]{:S(2)}) copy-start(s32[1024,1]{0,1:T(1,128)} %param.10) | copy-start | bytes 12292
  303.8 26.6 %all-to-all-start.1 = ((f32[8,2,512]{0,1,2:T(2,128)}), f32[8,2,512]{0,1,2:T(2,128)S(1)}, u32[]{:S(2)}, u32[]{:S(2)}) async-start(f32[8,2,512]{0,1,2:T(2,128)} %copy.20), calls=%async_computation.1 | async-start | bytes 1048576 | tf_op jit(solution)/shard_map/all_to_all | solution.py:133
  330.8 7.2 %copy-start.1 = (bf16[4,1024,384]{2,1,0:T(8,128)(2,1)S(1)}, bf16[4,1024,384]{2,1,0:T(8,128)(2,1)}, u32[]{:S(2)}) copy-start(bf16[4,1024,384]{2,1,0:T(8,128)(2,1)} %param.8) | copy-start | bytes 9437188
where the time goes:
time: 341 us; the launch traced here: 338 us
  other arithmetic  110 us (32%)
  waiting for transfers between devices  75.4 us (22%)
  local copies, waits for them, and re-layouts  62.4 us (18%)
  loops' own time  33.4 us (10%)
  matrix products  26.2 us (8%)
  starting transfers between devices  22.3 us (7%)
  blocking collectives  8.29 us (2%)
    all_to_all x1, waiting for transfers between devices, body(): lax.all_to_all(picked, 'row', split_axis=1, concat_axis=2, tiled=True)  74.9 us
    select_n x1, other arithmetic, pick_blocks(): jnp.where(matched, values[..., block_id * PIX_BLK:(block_id + 1) * PIX_BL...  22 us
    reduce_sum x8, other arithmetic, compute_live(): jnp.sum((real_part * cosine_t + imag_part * sine_t) * weight[None, :], ax...  19.8 us
    select_n x1, other arithmetic, component_tables(): first_table = jnp.where(band_index == 0, cosine_x, sine_x)  19.5 us
    another operation x1, loops' own time, body(): partial_psi = lax.map(trotter, slots_own)  19.1 us
    another operation x1, other arithmetic  17.1 us
    all_to_all x1, starting transfers between devices, body(): lax.all_to_all(picked, 'row', split_axis=1, concat_axis=2, tiled=True)  15.7 us
    another operation x8, loops' own time, trotter(): return lax.cond(counts_own[freq_slot] > 0, compute_live, give_zeros, 0)  14.3 us
  transfers between devices with their start and end apart: 2, of which 2 were waited for; matrix products, arithmetic and copies ran while one was open for 12% of the time, Pallas kernels for 0%

commit v1 on v0

v1 whole, which is shorter than its diff:
```python
import math

import jax
import jax.numpy as jnp
import ml_dtypes
import numpy as np
from jax import lax
from jax.experimental import pallas as pl
from jax.experimental.pallas import tpu as pltpu
from jax.sharding import Mesh
from jax.sharding import PartitionSpec as P

NX = 1024
NY = 512
PIX_BLK = 128
BLK_BAND = 3
PIX_BAND = PIX_BLK * BLK_BAND
ROWS_DEV = 4
CAP = 2
HALF_X = NX // 2
CHUNK = 256
STEPS = HALF_X // CHUNK
GROUP = ROWS_DEV * PIX_BLK
DEPTH = BLK_BAND * GROUP
TALL = NY + 16
GRID_Z, GRID_XH, GRID_Y, GRID_CORE, GRID_BAND = 8, 2, 4, 2, 2
ROW_AXES = ("z", "xh", "y", "core")
F32, BF16 = jnp.float32, jnp.bfloat16


def forward_table():
    turns = np.outer(np.arange(HALF_X + 1), np.arange(NX)) % NX
    angle = turns.astype(np.float32) * np.float32(2.0 * math.pi / NX)
    norm_factor = np.float32(1.0 / math.sqrt(NX))
    cosine, sine = np.cos(angle) * norm_factor, np.sin(angle) * norm_factor
    lower = -sine[:HALF_X]
    lower[0] = cosine[HALF_X]
    pieces = np.stack(
        [cosine[:HALF_X].reshape(STEPS, CHUNK, NX), lower.reshape(STEPS, CHUNK, NX)], axis=1
    )
    return pieces.reshape(NX, NX).astype(ml_dtypes.bfloat16)


def backward_table():
    turns = np.outer(np.arange(HALF_X + 1), np.arange(NX)) % NX
    angle = turns.astype(np.float64) * (2.0 * math.pi / NX)
    scale = 1.0 / math.sqrt(NX) / math.sqrt(GRID_BAND * CAP * PIX_BLK)
    upper = np.cos(angle[:HALF_X]) * scale
    upper[0] *= 0.5
    lower = -np.sin(angle[:HALF_X]) * scale
    lower[0] = np.cos(angle[HALF_X]) * scale
    pieces = np.stack(
        [upper.reshape(STEPS, CHUNK, NX), lower.reshape(STEPS, CHUNK, NX)], axis=1
    )
    whole = pieces.reshape(NX, NX).astype(np.float32)
    high = whole.astype(ml_dtypes.bfloat16)
    low = (whole - high.astype(np.float32)).astype(ml_dtypes.bfloat16)
    return high, low


def horner(variable, coefficients):
    total = jnp.full_like(variable, coefficients[-1])
    for coefficient in coefficients[-2::-1]:
        total = total * variable + coefficient
    return total


SINE = [(-1.0) ** k / math.factorial(2 * k + 1) for k in range(8)]
COSINE = [(-1.0) ** k / math.factorial(2 * k) for k in range(8)]


def small_sincos(angle):
    square = angle * angle
    return angle * horner(square, SINE), horner(square, COSINE)


def cycles_sincos(cycles):
    cycles = cycles - jnp.round(cycles)
    sine, cosine = small_sincos(cycles * math.pi)
    return 2.0 * sine * cosine, 1.0 - 2.0 * sine * sine


def local_kernel(
    place_ref,
    masks_ref,
    gradient_ref,
    table_ref,
    intens_ref,
    keep_ref,
    send_ref,
    values,
    shift_base,
    shift_table,
    coarse,
    fine,
    phase,
    rotated,
    lone,
    products,
    lone_out,
    copy_sem,
):
    step = pl.program_id(0)
    own_row = place_ref[0]
    own_core = place_ref[1]

    def copies():
        for block in range(BLK_BAND):
            for row in range(ROWS_DEV):
                yield pltpu.make_async_copy(
                    intens_ref.at[row, :, pl.ds(block * PIX_BLK, PIX_BLK)],
                    values.at[:, pl.ds(block * GROUP + row * PIX_BLK, PIX_BLK)],
                    copy_sem.at[block * ROWS_DEV + row],
                )

    @pl.when(step == 0)
    def prepare():
        for copy in copies():
            copy.start()
        gradient_x = gradient_ref[0:1, :]
        gradient_y = gradient_ref[1:2, :]
        nearest = jnp.round(gradient_y)
        rest = gradient_y - nearest
        sinc = horner(
            rest * rest, [SINE[k] * math.pi ** (2 * k) for k in range(8)]
        )
        small = rest * (math.pi / NY)
        peak = sinc * (1.0 - small * small * (1.0 / 3.0))
        parity = nearest - 2.0 * jnp.floor(nearest * 0.5)
        lobes = (1.0 - 2.0 * parity) * (rest * math.pi) * sinc * (1.0 / NY)
        sine_g, cosine_g = small_sincos(gradient_y * (math.pi / NY))
        index = lax.broadcasted_iota(jnp.int32, (TALL, PIX_BLK), 0)
        offset = index - (ROWS_DEV - 1) - ROWS_DEV * own_row
        distance = offset.astype(F32)
        folded = distance - NY * jnp.round(distance * (1.0 / NY))
        sine_d, cosine_d = small_sincos(folded * (math.pi / NY))
        row_sign = (1 - 2 * (offset & 1)).astype(F32)
        for block in range(BLK_BAND):
            lanes = slice(block * PIX_BLK, (block + 1) * PIX_BLK)
            upper = (cosine_d * cosine_g[:, lanes] + sine_d * sine_g[:, lanes]) * row_sign
            lower = sine_d * cosine_g[:, lanes] - cosine_d * sine_g[:, lanes]
            turns = (distance - nearest[:, lanes]) * (1.0 / NY)
            at_peak = turns == jnp.round(turns)
            lower = jnp.where(at_peak, 1.0, lower)
            shift_base[:, lanes] = jnp.where(
                at_peak, peak[:, lanes], -lobes[:, lanes] * upper / lower
            )
        first_row = lax.broadcasted_iota(jnp.int32, (TALL - NY, PIX_BLK), 0) == 0
        for block in range(BLK_BAND):
            lanes = slice(block * PIX_BLK, (block + 1) * PIX_BLK)
            for row in range(ROWS_DEV):
                column = block * GROUP + row * PIX_BLK
                start = ROWS_DEV - 1 - row
                shift_table[0:NY, column : column + PIX_BLK] = shift_base[
                    start : start + NY, lanes
                ].astype(BF16)
                shift_table[NY:TALL, column : column + PIX_BLK] = jnp.where(
                    first_row, lobes[:, lanes] * (1.0 - 2.0 * (row % 2)), 0.0
                ).astype(BF16)
        eights = lax.broadcasted_iota(jnp.int32, (HALF_X // 8, PIX_BAND), 0).astype(F32)
        coarse[0], coarse[1] = cycles_sincos(gradient_x * (eights * (8.0 / NX)))
        units = lax.broadcasted_iota(jnp.int32, (8, PIX_BAND), 0).astype(F32)
        fine[0], fine[1] = cycles_sincos(gradient_x * (units * (1.0 / NX)))
        lone[...] = jnp.zeros_like(lone)
        for copy in copies():
            copy.wait()

    for octet in range(CHUNK // 8):
        at_octet = pl.ds(step * (CHUNK // 8) + octet, 1)
        sine_c, cosine_c = coarse[0, at_octet, :], coarse[1, at_octet, :]
        rows = slice(octet * 8, octet * 8 + 8)
        phase[0, rows, :] = sine_c * fine[1] + cosine_c * fine[0]
        phase[1, rows, :] = cosine_c * fine[1] - sine_c * fine[0]

    contract_last = (((1,), (1,)), ((), ()))
    for block in range(BLK_BAND):
        columns = slice(block * GROUP, (block + 1) * GROUP)
        lanes = slice(block * PIX_BLK, (block + 1) * PIX_BLK)
        spectrum = jnp.dot(table_ref[...], values[:, columns], preferred_element_type=F32)
        spectrum = spectrum.astype(BF16).astype(F32)
        sine_p, cosine_p = phase[0, :, lanes], phase[1, :, lanes]
        for row in range(ROWS_DEV):
            inner = slice(row * PIX_BLK, (row + 1) * PIX_BLK)
            outer = slice(block * GROUP + row * PIX_BLK, block * GROUP + (row + 1) * PIX_BLK)
            real_part = spectrum[:CHUNK, inner]
            imag_part = spectrum[CHUNK:, inner]
            rotated[:CHUNK, outer] = (real_part * cosine_p + imag_part * sine_p).astype(BF16)
            rotated[CHUNK:, outer] = (imag_part * cosine_p - real_part * sine_p).astype(BF16)

        @pl.when(step == 0)
        def middle():
            sine_m, cosine_m = cycles_sincos(gradient_ref[0:1, lanes] * 0.5)
            weight = masks_ref[2 * BLK_BAND + block : 2 * BLK_BAND + block + 1, 0:PIX_BLK]
            top = lax.broadcasted_iota(jnp.int32, (16, PIX_BLK), 0) == 0
            for row in range(ROWS_DEV):
                inner = slice(row * PIX_BLK, (row + 1) * PIX_BLK)
                outer = slice(block * GROUP + row * PIX_BLK, block * GROUP + (row + 1) * PIX_BLK)
                only = spectrum[CHUNK : CHUNK + 1, inner] * weight
                lone[0:16, outer] = jnp.where(top, only * cosine_m, 0.0).astype(BF16)
                lone[PIX_BLK : PIX_BLK + 16, outer] = jnp.where(
                    top, only * sine_m, 0.0
                ).astype(BF16)

        products[block] = lax.dot_general(
            shift_table[:, columns],
            rotated[:, columns],
            contract_last,
            preferred_element_type=F32,
        )

    @pl.when(step == 0)
    def middle_out():
        both = lax.dot_general(
            shift_table[...], lone[...], contract_last, preferred_element_type=F32
        )
        even = (lax.broadcasted_iota(jnp.int32, (NY, PIX_BLK), 0) & 1) == 0
        one = both[NY : NY + 1, PIX_BLK:]
        lone_out[0] = both[:NY, :PIX_BLK] - jnp.where(even, one, -one)
        one = both[NY : NY + 1, :PIX_BLK]
        lone_out[1] = both[:NY, PIX_BLK:] + jnp.where(even, one, -one)

    sums = masks_ref[0:BLK_BAND, pl.ds(step * CHUNK, CHUNK)]
    differences = masks_ref[BLK_BAND : 2 * BLK_BAND, pl.ds(step * CHUNK, CHUNK)]
    edge = jnp.zeros((4, CHUNK), F32)
    sum_edge_real = sum_edge_imag = diff_edge_real = diff_edge_imag = edge[0:1]
    for block in range(BLK_BAND):
        edge_real = products[block, NY : NY + 1, :CHUNK]
        edge_imag = products[block, NY : NY + 1, CHUNK:]
        sum_edge_real = sum_edge_real + differences[block : block + 1] * edge_real
        sum_edge_imag = sum_edge_imag + differences[block : block + 1] * edge_imag
        diff_edge_real = diff_edge_real + sums[block : block + 1] * edge_real
        diff_edge_imag = diff_edge_imag + sums[block : block + 1] * edge_imag
    even = (lax.broadcasted_iota(jnp.int32, (8, CHUNK), 0) & 1) == 0
    alternating = jnp.where(even, 1.0, -1.0)
    add_hr = -alternating * sum_edge_imag
    add_hi = alternating * sum_edge_real
    add_gr = -alternating * diff_edge_imag
    add_gi = alternating * diff_edge_real
    lane_zero = (lax.broadcasted_iota(jnp.int32, (8, PIX_BLK), 1) == 0) & (step == 0)

    def tile(start):
        rows = slice(start, start + 8)
        herm_real, herm_imag, anti_real, anti_imag = add_hr, add_hi, add_gr, add_gi
        for block in range(BLK_BAND):
            real_part = products[block, rows, :CHUNK]
            imag_part = products[block, rows, CHUNK:]
            herm_real = herm_real + sums[block : block + 1] * real_part
            herm_imag = herm_imag + sums[block : block + 1] * imag_part
            anti_real = anti_real + differences[block : block + 1] * real_part
            anti_imag = anti_imag + differences[block : block + 1] * imag_part

        def mend(part, which):
            first = jnp.where(lane_zero, lone_out[which, rows, :], part[:, :PIX_BLK])
            return jnp.concatenate([first, part[:, PIX_BLK:]], axis=1)

        return (
            (herm_real, mend(herm_imag, 0)),
            (anti_imag, mend(-anti_real, 1)),
        )

    upper_rows = lax.broadcasted_iota(jnp.int32, (8, CHUNK), 0) < ROWS_DEV
    first_core = jnp.full((8, CHUNK), own_core, jnp.int32) == 0

    def split_pair(left, right):
        low = jnp.where(upper_rows, left, pltpu.roll(right, ROWS_DEV, 0))
        high = jnp.where(upper_rows, pltpu.roll(left, ROWS_DEV, 0), right)
        return jnp.where(first_core, low, high), jnp.where(first_core, high, low)

    for x_high in range(GRID_XH):
        for y_at in range(GRID_Y):
            for quad in range(GRID_Z // 4):
                pairs = []
                for pair in range(2):
                    z_at = quad * 4 + pair * 2
                    start = z_at * 64 + x_high * 32 + y_at * 8
                    pairs.append((tile(start), tile(start + 64)))
                target = x_high * 128 + y_at * 32 + quad * 16
                rows = slice(target, target + 16)
                for band in range(GRID_BAND):
                    for part in range(2):
                        lanes = slice(part * CHUNK, (part + 1) * CHUNK)
                        kept, sent = [], []
                        for left, right in pairs:
                            own, other = split_pair(left[band][part], right[band][part])
                            kept.append(own)
                            sent.append(other)
                        keep_ref[band, rows, lanes] = jnp.concatenate(kept, axis=0).astype(BF16)
                        send_ref[band, rows, lanes] = jnp.concatenate(sent, axis=0).astype(BF16)


def local_part(place, masks, gradient, table, intens):
    out_block = pl.BlockSpec((GRID_BAND, NY // 2, 2 * CHUNK), lambda i: (0, 0, i))
    out_shape = jax.ShapeDtypeStruct((GRID_BAND, NY // 2, NX), BF16)
    return pl.pallas_call(
        local_kernel,
        grid=(STEPS,),
        in_specs=[
            pl.BlockSpec(memory_space=pltpu.SMEM),
            pl.BlockSpec((16, HALF_X), lambda i: (0, 0)),
            pl.BlockSpec((2, PIX_BAND), lambda i: (0, 0)),
            pl.BlockSpec((2 * CHUNK, NX), lambda i: (i, 0)),
            pl.BlockSpec(memory_space=pl.ANY),
        ],
        out_specs=[out_block, out_block],
        out_shape=[out_shape, out_shape],
        scratch_shapes=[
            pltpu.VMEM((NX, DEPTH), BF16),
            pltpu.VMEM((TALL, PIX_BAND), F32),
            pltpu.VMEM((TALL, DEPTH), BF16),
            pltpu.VMEM((2, HALF_X // 8, PIX_BAND), F32),
            pltpu.VMEM((2, 8, PIX_BAND), F32),
            pltpu.VMEM((2, CHUNK, PIX_BAND), F32),
            pltpu.VMEM((2 * CHUNK, DEPTH), BF16),
            pltpu.VMEM((2 * PIX_BLK, DEPTH), BF16),
            pltpu.VMEM((BLK_BAND, TALL, 2 * CHUNK), F32),
            pltpu.VMEM((2, NY, PIX_BLK), F32),
            pltpu.SemaphoreType.DMA((BLK_BAND * ROWS_DEV,)),
        ],
        compiler_params=pltpu.CompilerParams(vmem_limit_bytes=48 * 1024 * 1024),
    )(place, masks, gradient, table, intens)


def final_kernel(parts_ref, high_ref, low_ref, image_ref):
    total = parts_ref[0].astype(F32)
    for source in range(1, GRID_Z):
        total = total + parts_ref[source].astype(F32)
    high = total.astype(BF16)
    low = (total - high.astype(F32)).astype(BF16)
    image = jnp.dot(high, high_ref[...], preferred_element_type=F32)
    image = image + jnp.dot(low, high_ref[...], preferred_element_type=F32)
    image_ref[0] = image + jnp.dot(high, low_ref[...], preferred_element_type=F32)


def final_part(parts, high, low):
    return pl.pallas_call(
        final_kernel,
        out_shape=jax.ShapeDtypeStruct((1, ROWS_DEV, NX), F32),
        compiler_params=pltpu.CompilerParams(vmem_limit_bytes=32 * 1024 * 1024),
    )(parts, high, low)


def used_masks(block_list, block_count):
    block_ids = jnp.arange(BLK_BAND, dtype=jnp.int32)[:, None, None]
    live = jnp.arange(CAP, dtype=jnp.int32)[None, :] < block_count
    used = jnp.any((block_list[None] == block_ids) & live[None], axis=-1).astype(F32)
    mirror = jnp.concatenate([used[:, :1], used[:, :HALF_X:-1]], axis=1)
    ahead = used[:, :HALF_X]
    middle = jnp.broadcast_to(used[:, HALF_X : HALF_X + 1], (BLK_BAND, HALF_X))
    spare = jnp.zeros((16 - 3 * BLK_BAND, HALF_X), F32)
    return jnp.concatenate([ahead + mirror, ahead - mirror, middle, spare], axis=0)


def body(intens, block_list, block_count, pixel_gradient):
    own_row = lax.axis_index(ROW_AXES)
    own_core = lax.axis_index("core")
    place = jnp.stack([own_row, own_core]).astype(jnp.int32)
    masks = used_masks(block_list, block_count)
    keep, send = local_part(
        place, masks, pixel_gradient, jnp.asarray(forward_table()), intens
    )
    received = lax.ppermute(send, "core", [(0, 1), (1, 0)])
    chip = (keep.astype(F32) + received.astype(F32)).astype(BF16)
    chip = chip.reshape(GRID_BAND * GRID_XH * GRID_Y, 4 * GRID_Z, NX)
    spread = lax.all_to_all(
        chip, ("band", "xh", "y"), split_axis=0, concat_axis=0, tiled=True
    )
    plane = jnp.sum(spread.astype(F32), axis=0).astype(BF16)
    plane = plane.reshape(GRID_Z, ROWS_DEV, NX)
    parts = lax.all_to_all(plane, "z", split_axis=0, concat_axis=0, tiled=True)
    high, low = backward_table()
    return final_part(parts, jnp.asarray(high), jnp.asarray(low))


def solution(mesh):
    grid = Mesh(
        mesh.devices.reshape(GRID_Z, GRID_XH, GRID_Y, GRID_CORE, GRID_BAND),
        ROW_AXES + ("band",),
    )
    return jax.shard_map(
        body,
        mesh=grid,
        in_specs=(P(ROW_AXES, None, "band"), P(None, "band"), P(None, "band"), P(None, "band")),
        out_specs=P("band", ROW_AXES, None),
        check_vma=False,
    )
```

time: 341 us -> 63.5 us (0.19)
  other arithmetic: 110 us -> 2.27 us
  waiting for transfers between devices: 75.4 us -> 2.65 us
  local copies, waits for them, and re-layouts: 62.4 us -> 4.68 us
  loops' own time: 33.4 us -> 0 us
  blocking collectives: 8.29 us -> 39.7 us
  matrix products: 26.2 us -> 0 us
  starting transfers between devices: 22.3 us -> 0.09 us
  Pallas kernels: 0 us -> 13.7 us
    all_to_all x2 -> x0, waiting for transfers between devices: 75.4 us -> none  [the longest x1 74.9 us: body(): lax.all_to_all(picked, 'row', split_axis=1, concat_axis=2, tiled=True)]
    select_n x11 -> x0, other arithmetic: 41.6 us -> none  [the longest x1 22 us: pick_blocks(): jnp.where(matched, values[..., block_id * PIX_BLK:(block_id + 1) * PIX_BL...]
    all_to_all x0 -> x2, blocking collectives: none -> 39.7 us  [the longest x1 23.1 us: body(): lax.all_to_all(chip, ('band', 'xh', 'y'), split_axis=0, concat_axis=0, ti...]
    another operation x9 -> x0, loops' own time: 33.4 us -> none  [the longest x1 19.1 us: body(): partial_psi = lax.map(trotter, slots_own)]
    dynamic_slice x40 -> x0, local copies, waits for them, and re-layouts: 27.4 us -> none  [the longest x8 8.68 us: compute_live(): lax.dynamic_index_in_dim(received, freq_slot, 1, keepdims=False)]
    dot_general x11 -> x0, matrix products: 26.2 us -> none  [the longest x1 7.31 us: body(): jnp.einsum('fx,rxp->frp', table_x, intens, preferred_element_type=jnp.flo...]
    all_to_all x2 -> x0, starting transfers between devices: 22.3 us -> none  [the longest x1 15.7 us: body(): lax.all_to_all(picked, 'row', split_axis=1, concat_axis=2, tiled=True)]
    reduce_sum x8 -> x1, other arithmetic: 19.8 us -> 0.2 us  [body(): plane = jnp.sum(spread.astype(F32), axis=0).astype(BF16)]
  transfers between devices with their start and end apart: 2 -> 1, of which waited for: 2 -> 1; matrix products, arithmetic and copies ran while one was open for 12% -> 0% of each run, Pallas kernels for 0% -> 0%
where the time goes in v1:
time: 63.5 us; the launch traced here: 63.2 us
  blocking collectives  39.7 us (63%)
  Pallas kernels  13.7 us (22%)
  local copies, waits for them, and re-layouts  4.68 us (7%)
  waiting for transfers between devices  2.65 us (4%)
  other arithmetic  2.27 us (4%)
    all_to_all x1, blocking collectives, body(): lax.all_to_all(chip, ('band', 'xh', 'y'), split_axis=0, concat_axis=0, ti...  23.1 us
    all_to_all x1, blocking collectives, body(): parts = lax.all_to_all(plane, 'z', split_axis=0, concat_axis=0, tiled=True)  16.6 us
    pallas_call x1, Pallas kernels, local_part(): pl.pallas_call(local_kernel, grid=(STEPS,), in_specs=[pl.BlockSpec(memory...  12.1 us
    unnamed x10, local copies, waits for them, and re-layouts  4.31 us
    ppermute x1, waiting for transfers between devices, body(): received = lax.ppermute(send, 'core', [(0, 1), (1, 0)])  2.65 us
    pallas_call x1, Pallas kernels, final_part(): pl.pallas_call(final_kernel, out_shape=jax.ShapeDtypeStruct((1, ROWS_DEV,...  1.53 us
  transfers between devices with their start and end apart: 1, of which 1 were waited for; matrix products, arithmetic and copies ran while one was open for 0% of the time, Pallas kernels for 0%

profile of v1, /device:TPU:2, one launch (start us, length us, event | category | flops | bytes accessed | tf_op | source)
XLA Modules:
  0.0 63.2 jit_solution(4958228525714349544)
XLA Ops:
  0.0 0.7 %iota_compare_fusion = pred[1024,2]{0,1:T(4,128)(4,1)S(1)} fusion(s32[1024]{0:T(1024)} %bitcast.7), kind=kLoop, calls=%fused_computation.4 | loop fusion | flops 2048 | bytes 6144 | tf_op jit(solution)/shard_map/lt | solution.py:344
  0.7 0.7 %and_reduce_fusion = pred[3,1024]{1,0:T(4,128)(4,1)S(1)} fusion(pred[1024,2]{0,1:T(4,128)(4,1)S(1)} %iota_compare_fusion, s32[1024,2]{0,1:T(2,128)} %param.8), kind=kLoop, calls=%fused_computation.1 | loop fusion | flops 15360 | bytes 13312 | tf_op jit(solution)/shard_map/reduce_or | solution.py:345
  1.5 0.1 slice_reduce_fusion
  1.6 0.1 slice.18
  1.6 0.1 pad.3.clone
  1.7 0.1 pad.2.clone
  1.8 0.4 reverse
  2.2 0.1 slice.23
  2.2 0.1 pad_add_fusion.place_ref
  2.3 0.1 slice_add_fusion
  2.4 0.1 maximum_maximum_fusion.masks_ref
  2.5 0.0 copy-start.2
  2.5 1.6 %copy-done.2 = bf16[1024,1024]{1,0:T(8,128)(2,1)S(1)} copy-done((bf16[1024,1024]{1,0:T(8,128)(2,1)S(1)}, bf16[1024,1024]{1,0:T(8,128)(2,1)}, u32[]{:S(2)}) %copy-start.2) | copy-done | bytes 2097176
  4.1 0.0 copy-start.3
  4.1 0.7 %copy-done.3 = f32[2,384]{1,0:T(2,128)S(1)} copy-done((f32[2,384]{1,0:T(2,128)S(1)}, f32[2,384]{1,0:T(2,128)}, u32[]{:S(2)}) %copy-start.3) | copy-done | bytes 3096
  4.7 12.1 %shard_map.73 = (bf16[2,256,1024]{2,1,0:T(8,128)(2,1)S(1)}, bf16[2,256,1024]{2,1,0:T(8,128)(2,1)S(1)}) custom-call(s32[2]{0:T(128)S(1)} %pad_add_fusion.place_ref, f32[16,512]{1,0:T(8,128)S(1)} %maximum_maximum_fusion.masks_ref, f32[2,384]{1,0:T(2,128)S(1)} %copy-done.3, bf16[1024,1024]{1,0:T(8,128)(2,1)S(1)} %copy-done.2, bf16[4,1024,384]{2,1,0:T(8,128)(2,1)} %intens_ref.1), custom_call_target="tpu_custom_call" | custom-call | tf_op jit(solution)/shard_map/pallas_call | solution.py:294
  16.9 0.1 collective-permute-start
  17.0 2.6 %collective-permute-done = bf16[2,256,1024]{2,1,0:T(8,128)(2,1)S(1)} collective-permute-done((bf16[2,256,1024]{2,1,0:T(8,128)(2,1)S(1)}, bf16[2,256,1024]{2,1,0:T(8,128)(2,1)S(1)}, u32[]{:S(2)}, u32[]{:S(2)}) %collective-permute-start) | collective-permute-done | bytes 1048608 | tf_op jit(solution)/shard_map/ppermute | solution.py:361
  19.6 0.4 add_convert_fusion
  20.0 0.0 copy-start
  20.1 23.1 %all_to_all.10 = bf16[16,32,1024]{2,1,0:T(8,128)(2,1)S(1)} all-to-all(bf16[16,32,1024]{2,1,0:T(8,128)(2,1)S(1)} %bitcast.5), channel_id=1, replica_groups=mesh['z'=8,'xh'=2,'y'=4,'core'=2,'band'=2] {'band','xh','y'}, dimensions={0} | all-to-all | bytes 2097152 | tf_op jit(solution)/shard_map/all_to_all | solution.py:364
  43.2 0.2 reduce_sum.12
  43.4 16.6 %all_to_all.11.parts_ref = bf16[8,4,1024]{2,1,0:T(4,128)(2,1)S(1)} all-to-all(bf16[8,4,1024]{2,1,0:T(4,128)(2,1)S(1)} %reshape.28), channel_id=1, replica_groups=mesh['z'=8,'xh'=2,'y'=4,'core'=2,'band'=2] {'z'}, dimensions={0} | all-to-all | bytes 131072 | tf_op jit(solution)/shard_map/all_to_all | solution.py:369
  60.0 0.0 copy-done
  60.0 0.0 copy-start.1
  60.0 1.6 %copy-done.1 = bf16[1024,1024]{1,0:T(8,128)(2,1)S(1)} copy-done((bf16[1024,1024]{1,0:T(8,128)(2,1)S(1)}, bf16[1024,1024]{1,0:T(8,128)(2,1)}, u32[]{:S(2)}) %copy-start.1) | copy-done | bytes 2097176
  61.6 1.5 %shard_map.74 = f32[1,4,1024]{2,1,0:T(4,128)} custom-call(bf16[8,4,1024]{2,1,0:T(4,128)(2,1)S(1)} %all_to_all.11.parts_ref, bf16[1024,1024]{1,0:T(8,128)(2,1)S(1)} %copy-done.1, bf16[1024,1024]{1,0:T(8,128)(2,1)S(1)} %copy-done), custom_call_target="tpu_custom_call" | custom-call | tf_op jit(solution)/shard_map/pallas_call | solution.py:335
  (3 shorter events, 0.0 us)
Async XLA Ops:
  2.5 1.6 %copy-start.2 = (bf16[1024,1024]{1,0:T(8,128)(2,1)S(1)}, bf16[1024,1024]{1,0:T(8,128)(2,1)}, u32[]{:S(2)}) copy-start(bf16[1024,1024]{1,0:T(8,128)(2,1)} %constant.38.clone.table_ref) | copy-start | bytes 6291460
  4.1 0.7 %copy-start.3 = (f32[2,384]{1,0:T(2,128)S(1)}, f32[2,384]{1,0:T(2,128)}, u32[]{:S(2)}) copy-start(f32[2,384]{1,0:T(2,128)} %gradient_ref.1) | copy-start | bytes 9220
  16.9 2.7 %collective-permute-start = (bf16[2,256,1024]{2,1,0:T(8,128)(2,1)S(1)}, bf16[2,256,1024]{2,1,0:T(8,128)(2,1)S(1)}, u32[]{:S(2)}, u32[]{:S(2)}) collective-permute-start(bf16[2,256,1024]{2,1,0:T(8,128)(2,1)S(1)} %get-tuple-element.8), channel_id=1, source_target_pairs={{0,2},{2,0},{1,3},{3,1},{4,6},{6,4},{5,7},{7,5},{8,10},{10,8},{9,1... | collective-permute-start | bytes 3145736 | tf_op jit(solution)/shard_map/ppermute | solution.py:361
  20.0 40.0 %copy-start = (bf16[1024,1024]{1,0:T(8,128)(2,1)S(1)}, bf16[1024,1024]{1,0:T(8,128)(2,1)}, u32[]{:S(2)}) copy-start(bf16[1024,1024]{1,0:T(8,128)(2,1)} %constant.40.clone.low_ref) | copy-start | bytes 6291460
  60.0 1.6 %copy-start.1 = (bf16[1024,1024]{1,0:T(8,128)(2,1)S(1)}, bf16[1024,1024]{1,0:T(8,128)(2,1)}, u32[]{:S(2)}) copy-start(bf16[1024,1024]{1,0:T(8,128)(2,1)} %constant.39.clone.high_ref) | copy-start | bytes 6291460

commit v2 on v0

v2 whole, which is shorter than its diff:
```python
import math

import jax
import jax.numpy as jnp
import ml_dtypes
import numpy as np
from jax import lax
from jax.experimental import pallas as pl
from jax.experimental.pallas import tpu as pltpu
from jax.sharding import Mesh
from jax.sharding import PartitionSpec as P

NX = 1024
NY = 512
PIX_BLK = 128
BLK_BAND = 3
PIX_BAND = PIX_BLK * BLK_BAND
ROWS_DEV = 4
CAP = 2
HALF_X = NX // 2
CHUNK = 256
STEPS = HALF_X // CHUNK
GROUP = ROWS_DEV * PIX_BLK
DEPTH = BLK_BAND * GROUP
TALL = NY + 16
GRID_Z, GRID_XH, GRID_Y, GRID_CORE, GRID_BAND = 8, 2, 4, 2, 2
PIECES = GRID_XH * GRID_Y * GRID_BAND
ROW_AXES = ("z", "xh", "y", "core")
F32, BF16 = jnp.float32, jnp.bfloat16


def forward_table():
    turns = np.outer(np.arange(HALF_X + 1), np.arange(NX)) % NX
    angle = turns.astype(np.float32) * np.float32(2.0 * math.pi / NX)
    norm_factor = np.float32(1.0 / math.sqrt(NX))
    cosine, sine = np.cos(angle) * norm_factor, np.sin(angle) * norm_factor
    lower = -sine[:HALF_X]
    lower[0] = cosine[HALF_X]
    pieces = np.stack(
        [cosine[:HALF_X].reshape(STEPS, CHUNK, NX), lower.reshape(STEPS, CHUNK, NX)], axis=1
    )
    return pieces.reshape(NX, NX).astype(ml_dtypes.bfloat16)


def backward_table():
    turns = np.outer(np.arange(HALF_X + 1), np.arange(NX)) % NX
    angle = turns.astype(np.float64) * (2.0 * math.pi / NX)
    scale = 1.0 / math.sqrt(NX) / math.sqrt(GRID_BAND * CAP * PIX_BLK)
    upper = np.cos(angle[:HALF_X]) * scale
    upper[0] *= 0.5
    lower = -np.sin(angle[:HALF_X]) * scale
    lower[0] = np.cos(angle[HALF_X]) * scale
    pieces = np.stack(
        [upper.reshape(STEPS, CHUNK, NX), lower.reshape(STEPS, CHUNK, NX)], axis=1
    )
    whole = pieces.reshape(NX, NX).astype(np.float32)
    high = whole.astype(ml_dtypes.bfloat16)
    low = (whole - high.astype(np.float32)).astype(ml_dtypes.bfloat16)
    return np.stack([high, low])


def horner(variable, coefficients):
    total = jnp.full_like(variable, coefficients[-1])
    for coefficient in coefficients[-2::-1]:
        total = total * variable + coefficient
    return total


SINE = [(-1.0) ** k / math.factorial(2 * k + 1) for k in range(8)]
COSINE = [(-1.0) ** k / math.factorial(2 * k) for k in range(8)]


def small_sincos(angle):
    square = angle * angle
    return angle * horner(square, SINE), horner(square, COSINE)


def cycles_sincos(cycles):
    cycles = cycles - jnp.round(cycles)
    sine, cosine = small_sincos(cycles * math.pi)
    return 2.0 * sine * cosine, 1.0 - 2.0 * sine * sine


def own_place():
    z_at, x_high, y_at, core = (lax.axis_index(name) for name in ROW_AXES)
    return ((z_at * GRID_XH + x_high) * GRID_Y + y_at) * GRID_CORE + core, core


def local_kernel(
    lists_hbm,
    counts_hbm,
    gradient_hbm,
    table_hbm,
    intens_hbm,
    keep_ref,
    send_ref,
    lists_ref,
    counts_ref,
    gradient_ref,
    table_ref,
    values,
    shift_base,
    shift_table,
    rotated,
    lone,
    products,
    lone_out,
    copy_sem,
):
    own_row, own_core = own_place()
    small_copies = [
        pltpu.make_async_copy(gradient_hbm, gradient_ref, copy_sem.at[0]),
        pltpu.make_async_copy(lists_hbm, lists_ref, copy_sem.at[1]),
        pltpu.make_async_copy(counts_hbm, counts_ref, copy_sem.at[2]),
    ]
    table_copies = []
    for step in range(STEPS):
        rows = pl.ds(step * 2 * CHUNK, 2 * CHUNK)
        table_copies.append(
            pltpu.make_async_copy(table_hbm.at[rows], table_ref.at[rows], copy_sem.at[3 + step])
        )
    block_copies = []
    for block in range(BLK_BAND):
        block_copies.append([])
        for row in range(ROWS_DEV):
            block_copies[block].append(
                pltpu.make_async_copy(
                    intens_hbm.at[row, :, pl.ds(block * PIX_BLK, PIX_BLK)],
                    values.at[:, pl.ds(block * GROUP + row * PIX_BLK, PIX_BLK)],
                    copy_sem.at[3 + STEPS + block * ROWS_DEV + row],
                )
            )
    for copy in small_copies:
        copy.start()
    table_copies[0].start()
    for copy in sum(block_copies, []):
        copy.start()
    for copy in table_copies[1:]:
        copy.start()
    for copy in small_copies:
        copy.wait()

    gradient_x = gradient_ref[0:1, :]
    gradient_y = gradient_ref[1:2, :]
    nearest = jnp.round(gradient_y)
    rest = gradient_y - nearest
    sinc = horner(rest * rest, [SINE[k] * math.pi ** (2 * k) for k in range(8)])
    small = rest * (math.pi / NY)
    peak = sinc * (1.0 - small * small * (1.0 / 3.0))
    parity = nearest - 2.0 * jnp.floor(nearest * 0.5)
    lobes = (1.0 - 2.0 * parity) * (rest * math.pi) * sinc * (1.0 / NY)
    sine_g, cosine_g = small_sincos(gradient_y * (math.pi / NY))
    index = lax.broadcasted_iota(jnp.int32, (TALL, PIX_BLK), 0)
    offset = index - (ROWS_DEV - 1) - ROWS_DEV * own_row
    distance = offset.astype(F32)
    folded = distance - NY * jnp.round(distance * (1.0 / NY))
    sine_d, cosine_d = small_sincos(folded * (math.pi / NY))
    row_sign = (1 - 2 * (offset & 1)).astype(F32)
    first_row = lax.broadcasted_iota(jnp.int32, (TALL - NY, PIX_BLK), 0) == 0
    for block in range(BLK_BAND):
        lanes = slice(block * PIX_BLK, (block + 1) * PIX_BLK)
        upper = (cosine_d * cosine_g[:, lanes] + sine_d * sine_g[:, lanes]) * row_sign
        lower = sine_d * cosine_g[:, lanes] - cosine_d * sine_g[:, lanes]
        turns = (distance - nearest[:, lanes]) * (1.0 / NY)
        at_peak = turns == jnp.round(turns)
        lower = jnp.where(at_peak, 1.0, lower)
        shift_base[:, lanes] = jnp.where(
            at_peak, peak[:, lanes], -lobes[:, lanes] * upper / lower
        )
        for row in range(ROWS_DEV):
            column = block * GROUP + row * PIX_BLK
            start = ROWS_DEV - 1 - row
            shift_table[0:NY, column : column + PIX_BLK] = shift_base[
                start : start + NY, lanes
            ].astype(BF16)
            shift_table[NY:TALL, column : column + PIX_BLK] = jnp.where(
                first_row, lobes[:, lanes] * (1.0 - 2.0 * (row % 2)), 0.0
            ).astype(BF16)

    eights = lax.broadcasted_iota(jnp.int32, (HALF_X // 8, PIX_BAND), 0).astype(F32)
    coarse_sine, coarse_cosine = cycles_sincos(gradient_x * (eights * (8.0 / NX)))
    units = lax.broadcasted_iota(jnp.int32, (8, PIX_BAND), 0).astype(F32)
    fine_sine, fine_cosine = cycles_sincos(gradient_x * (units * (1.0 / NX)))
    middle_sine, middle_cosine = cycles_sincos(gradient_x * 0.5)

    block_ids = lax.broadcasted_iota(jnp.int32, (8, NX), 0)
    counts = counts_ref[0:1, :]
    used = ((lists_ref[0:1, :] == block_ids) & (counts > 0)) | (
        (lists_ref[1:2, :] == block_ids) & (counts > 1)
    )
    used = used.astype(F32)
    place_sum = lax.broadcasted_iota(jnp.int32, (HALF_X, HALF_X), 0) + lax.broadcasted_iota(
        jnp.int32, (HALF_X, HALF_X), 1
    )
    reverse = (place_sum == HALF_X).astype(F32).astype(BF16)
    mirror = jnp.dot(used[:, HALF_X:].astype(BF16), reverse, preferred_element_type=F32)
    lane_first = lax.broadcasted_iota(jnp.int32, (8, HALF_X), 1) == 0
    ahead = used[:, :HALF_X]
    mirror = jnp.where(lane_first, ahead, mirror)
    every_sum = ahead + mirror
    every_difference = ahead - mirror

    contract_last = (((1,), (1,)), ((), ()))
    even = (lax.broadcasted_iota(jnp.int32, (8, CHUNK), 0) & 1) == 0
    alternating = jnp.where(even, 1.0, -1.0)
    upper_rows = lax.broadcasted_iota(jnp.int32, (8, PIX_BLK), 0) < ROWS_DEV
    first_core = jnp.full((8, PIX_BLK), own_core, jnp.int32) == 0
    lane_zero = lax.broadcasted_iota(jnp.int32, (8, PIX_BLK), 1) == 0
    lone[...] = jnp.zeros_like(lone)

    for step in range(STEPS):
        table_copies[step].wait()
        table = table_ref[step * 2 * CHUNK : (step + 1) * 2 * CHUNK, :]
        for block in range(BLK_BAND):
            columns = slice(block * GROUP, (block + 1) * GROUP)
            lanes = slice(block * PIX_BLK, (block + 1) * PIX_BLK)
            if step == 0:
                for copy in block_copies[block]:
                    copy.wait()
            spectrum = jnp.dot(table, values[:, columns], preferred_element_type=F32)
            spectrum = spectrum.astype(BF16).astype(F32)
            sines, cosines = [], []
            for octet in range(step * CHUNK // 8, (step + 1) * CHUNK // 8):
                sine_c = coarse_sine[octet : octet + 1, lanes]
                cosine_c = coarse_cosine[octet : octet + 1, lanes]
                sines.append(sine_c * fine_cosine[:, lanes] + cosine_c * fine_sine[:, lanes])
                cosines.append(cosine_c * fine_cosine[:, lanes] - sine_c * fine_sine[:, lanes])
            sine_p = jnp.concatenate(sines, axis=0)
            cosine_p = jnp.concatenate(cosines, axis=0)
            for row in range(ROWS_DEV):
                inner = slice(row * PIX_BLK, (row + 1) * PIX_BLK)
                outer = slice(
                    block * GROUP + row * PIX_BLK, block * GROUP + (row + 1) * PIX_BLK
                )
                real_part = spectrum[:CHUNK, inner]
                imag_part = spectrum[CHUNK:, inner]
                rotated[:CHUNK, outer] = (
                    real_part * cosine_p + imag_part * sine_p
                ).astype(BF16)
                rotated[CHUNK:, outer] = (
                    imag_part * cosine_p - real_part * sine_p
                ).astype(BF16)
                if step == 0:
                    weight = used[block : block + 1, HALF_X : HALF_X + 1]
                    top = lax.broadcasted_iota(jnp.int32, (16, PIX_BLK), 0) == 0
                    only = imag_part[0:1] * weight
                    lone[0:16, outer] = jnp.where(
                        top, only * middle_cosine[:, lanes], 0.0
                    ).astype(BF16)
                    lone[PIX_BLK : PIX_BLK + 16, outer] = jnp.where(
                        top, only * middle_sine[:, lanes], 0.0
                    ).astype(BF16)
            products[block] = lax.dot_general(
                shift_table[:, columns],
                rotated[:, columns],
                contract_last,
                preferred_element_type=F32,
            )

        if step == 0:
            both = lax.dot_general(
                shift_table[...], lone[...], contract_last, preferred_element_type=F32
            )
            flips = (lax.broadcasted_iota(jnp.int32, (NY, PIX_BLK), 0) & 1) == 0
            one = both[NY : NY + 1, PIX_BLK:]
            lone_out[0] = both[:NY, :PIX_BLK] - jnp.where(flips, one, -one)
            one = both[NY : NY + 1, :PIX_BLK]
            lone_out[1] = both[:NY, PIX_BLK:] + jnp.where(flips, one, -one)

        sums = every_sum[:, step * CHUNK : (step + 1) * CHUNK]
        differences = every_difference[:, step * CHUNK : (step + 1) * CHUNK]
        add_hr = add_hi = add_gr = add_gi = jnp.zeros((1, CHUNK), F32)
        for block in range(BLK_BAND):
            edge_real = products[block, NY : NY + 1, :CHUNK]
            edge_imag = products[block, NY : NY + 1, CHUNK:]
            add_hr = add_hr - differences[block : block + 1] * edge_imag
            add_hi = add_hi + differences[block : block + 1] * edge_real
            add_gr = add_gr - sums[block : block + 1] * edge_imag
            add_gi = add_gi + sums[block : block + 1] * edge_real
        add_hr, add_hi = alternating * add_hr, alternating * add_hi
        add_gr, add_gi = alternating * add_gr, alternating * add_gi

        for x_high in range(GRID_XH):
            for y_at in range(GRID_Y):
                for z_at in range(GRID_Z):
                    start = z_at * 64 + x_high * 32 + y_at * 8
                    rows = slice(start, start + 8)
                    herm_real, herm_imag, anti_real, anti_imag = add_hr, add_hi, add_gr, add_gi
                    for block in range(BLK_BAND):
                        real_part = products[block, rows, :CHUNK]
                        imag_part = products[block, rows, CHUNK:]
                        plus, minus = sums[block : block + 1], differences[block : block + 1]
                        herm_real = herm_real + plus * real_part
                        herm_imag = herm_imag + plus * imag_part
                        anti_real = anti_real + minus * real_part
                        anti_imag = anti_imag + minus * imag_part
                    for band in range(GRID_BAND):
                        tiles = []
                        for part in range(2):
                            if band == 0:
                                whole = herm_imag if part else herm_real
                            else:
                                whole = -anti_real if part else anti_imag
                            for lane in range(0, CHUNK, PIX_BLK):
                                tiles.append(whole[:, lane : lane + PIX_BLK])
                        if step == 0:
                            tiles[len(tiles) // 2] = jnp.where(
                                lane_zero, lone_out[band, rows, :], tiles[len(tiles) // 2]
                            )
                        kept, sent = [], []
                        for left, right in zip(tiles[::2], tiles[1::2]):
                            low = jnp.where(upper_rows, left, pltpu.roll(right, ROWS_DEV, 0))
                            high = jnp.where(upper_rows, pltpu.roll(left, ROWS_DEV, 0), right)
                            kept.append(jnp.where(first_core, low, high))
                            sent.append(jnp.where(first_core, high, low))
                        piece = (x_high * GRID_Y + y_at) * GRID_BAND + band
                        target = z_at * 32 + step * (CHUNK // 16)
                        where = slice(target, target + CHUNK // 16)
                        keep_ref[piece, where, :] = jnp.concatenate(kept, axis=0).astype(BF16)
                        send_ref[piece, where, :] = jnp.concatenate(sent, axis=0).astype(BF16)


def local_part(lists, counts, gradient, table, intens):
    out_shape = jax.ShapeDtypeStruct((PIECES, 32 * GRID_Z, PIX_BLK), BF16)
    vmem = pl.BlockSpec(memory_space=pltpu.VMEM)
    anywhere = pl.BlockSpec(memory_space=pl.ANY)
    return pl.pallas_call(
        local_kernel,
        in_specs=[anywhere] * 5,
        out_specs=[vmem, vmem],
        out_shape=[out_shape, out_shape],
        scratch_shapes=[
            pltpu.VMEM((CAP, NX), jnp.int32),
            pltpu.VMEM((1, NX), jnp.int32),
            pltpu.VMEM((2, PIX_BAND), F32),
            pltpu.VMEM((NX, NX), BF16),
            pltpu.VMEM((NX, DEPTH), BF16),
            pltpu.VMEM((TALL, PIX_BAND), F32),
            pltpu.VMEM((TALL, DEPTH), BF16),
            pltpu.VMEM((2 * CHUNK, DEPTH), BF16),
            pltpu.VMEM((2 * PIX_BLK, DEPTH), BF16),
            pltpu.VMEM((BLK_BAND, TALL, 2 * CHUNK), F32),
            pltpu.VMEM((2, NY, PIX_BLK), F32),
            pltpu.SemaphoreType.DMA((3 + STEPS + BLK_BAND * ROWS_DEV,)),
        ],
        compiler_params=pltpu.CompilerParams(vmem_limit_bytes=48 * 1024 * 1024),
    )(lists, counts, gradient, table, intens)


def plane_kernel(pieces_ref, plane_ref):
    total = pieces_ref[0].astype(F32)
    for source in range(1, PIECES):
        total = total + pieces_ref[source].astype(F32)
    plane_ref[...] = total.astype(BF16)


def plane_part(pieces):
    return pl.pallas_call(
        plane_kernel,
        out_shape=jax.ShapeDtypeStruct((32 * GRID_Z, PIX_BLK), BF16),
        compiler_params=pltpu.CompilerParams(vmem_limit_bytes=32 * 1024 * 1024),
    )(pieces)


def final_kernel(parts_ref, table_ref, image_ref):
    total = parts_ref[0].astype(F32)
    for source in range(1, GRID_Z):
        total = total + parts_ref[source].astype(F32)
    tiles = [total[at : at + ROWS_DEV] for at in range(0, 32, ROWS_DEV)]
    total = jnp.concatenate(tiles, axis=1)
    high = total.astype(BF16)
    low = total - high.astype(F32)
    both = jnp.concatenate([high.astype(F32), low], axis=0).astype(BF16)
    image = jnp.dot(both, table_ref[0], preferred_element_type=F32)
    image = image[:ROWS_DEV] + image[ROWS_DEV:]
    image_ref[0] = image + jnp.dot(high, table_ref[1], preferred_element_type=F32)


def final_part(parts, table):
    return pl.pallas_call(
        final_kernel,
        out_shape=jax.ShapeDtypeStruct((1, ROWS_DEV, NX), F32),
        compiler_params=pltpu.CompilerParams(vmem_limit_bytes=32 * 1024 * 1024),
    )(parts, table)


def body(intens, block_list, block_count, pixel_gradient):
    keep, send = local_part(
        block_list.T, block_count.T, pixel_gradient, jnp.asarray(forward_table()), intens
    )
    received = lax.ppermute(send, "core", [(0, 1), (1, 0)])
    chip = (keep.astype(F32) + received.astype(F32)).astype(BF16)
    pieces = lax.all_to_all(
        chip, ("xh", "y", "band"), split_axis=0, concat_axis=0, tiled=True
    )
    plane = plane_part(pieces).reshape(GRID_Z, 32, PIX_BLK)
    parts = lax.all_to_all(plane, "z", split_axis=0, concat_axis=0, tiled=True)
    return final_part(parts, jnp.asarray(backward_table()))


def solution(mesh):
    grid = Mesh(
        mesh.devices.reshape(GRID_Z, GRID_XH, GRID_Y, GRID_CORE, GRID_BAND),
        ROW_AXES + ("band",),
    )
    return jax.shard_map(
        body,
        mesh=grid,
        in_specs=(P(ROW_AXES, None, "band"), P(None, "band"), P(None, "band"), P(None, "band")),
        out_specs=P("band", ROW_AXES, None),
        check_vma=False,
    )
```

time: 341 us -> 60.6 us (0.18)
  other arithmetic: 110 us -> 0.28 us
  waiting for transfers between devices: 75.4 us -> 2.65 us
  local copies, waits for them, and re-layouts: 62.4 us -> 3.66 us
  loops' own time: 33.4 us -> 0 us
  blocking collectives: 8.29 us -> 40.3 us
  matrix products: 26.2 us -> 0 us
  starting transfers between devices: 22.3 us -> 0.09 us
  Pallas kernels: 0 us -> 13.3 us
    all_to_all x2 -> x0, waiting for transfers between devices: 75.4 us -> none  [the longest x1 74.9 us: body(): lax.all_to_all(picked, 'row', split_axis=1, concat_axis=2, tiled=True)]
    select_n x11 -> x0, other arithmetic: 41.6 us -> none  [the longest x1 22 us: pick_blocks(): jnp.where(matched, values[..., block_id * PIX_BLK:(block_id + 1) * PIX_BL...]
    all_to_all x0 -> x2, blocking collectives: none -> 40.3 us  [the longest x1 23.6 us: body(): lax.all_to_all(chip, ('xh', 'y', 'band'), split_axis=0, concat_axis=0, ti...]
    another operation x9 -> x0, loops' own time: 33.4 us -> none  [the longest x1 19.1 us: body(): partial_psi = lax.map(trotter, slots_own)]
    dynamic_slice x40 -> x0, local copies, waits for them, and re-layouts: 27.4 us -> none  [the longest x8 8.68 us: compute_live(): lax.dynamic_index_in_dim(received, freq_slot, 1, keepdims=False)]
    dot_general x11 -> x0, matrix products: 26.2 us -> none  [the longest x1 7.31 us: body(): jnp.einsum('fx,rxp->frp', table_x, intens, preferred_element_type=jnp.flo...]
    all_to_all x2 -> x0, starting transfers between devices: 22.3 us -> none  [the longest x1 15.7 us: body(): lax.all_to_all(picked, 'row', split_axis=1, concat_axis=2, tiled=True)]
    reduce_sum x8 -> x0, other arithmetic: 19.8 us -> none  [compute_live(): jnp.sum((real_part * cosine_t + imag_part * sine_t) * weight[None, :], ax...]
  transfers between devices with their start and end apart: 2 -> 1, of which waited for: 2 -> 1; matrix products, arithmetic and copies ran while one was open for 12% -> 0% of each run, Pallas kernels for 0% -> 0%
where the time goes in v2:
time: 60.6 us; the launch traced here: 60.3 us
  blocking collectives  40.3 us (67%)
  Pallas kernels  13.3 us (22%)
  local copies, waits for them, and re-layouts  3.66 us (6%)
  waiting for transfers between devices  2.65 us (4%)
    all_to_all x1, blocking collectives, body(): lax.all_to_all(chip, ('xh', 'y', 'band'), split_axis=0, concat_axis=0, ti...  23.6 us
    all_to_all x1, blocking collectives, body(): parts = lax.all_to_all(plane, 'z', split_axis=0, concat_axis=0, tiled=True)  16.6 us
    pallas_call x1, Pallas kernels, local_part(): pl.pallas_call(local_kernel, in_specs=[anywhere] * 5, out_specs=[vmem, vm...  11.9 us
    unnamed x10, local copies, waits for them, and re-layouts  3.66 us
    ppermute x1, waiting for transfers between devices, body(): received = lax.ppermute(send, 'core', [(0, 1), (1, 0)])  2.65 us
    pallas_call x1, Pallas kernels, final_part(): pl.pallas_call(final_kernel, out_shape=jax.ShapeDtypeStruct((1, ROWS_DEV,...  1.27 us
  transfers between devices with their start and end apart: 1, of which 1 were waited for; matrix products, arithmetic and copies ran while one was open for 0% of the time, Pallas kernels for 0%

profile of v2, /device:TPU:2, one launch (start us, length us, event | category | flops | bytes accessed | tf_op | source)
XLA Modules:
  0.0 60.3 jit_solution(9056542802934494119)
XLA Ops:
  0.0 0.0 copy-start.1
  0.0 1.6 %copy-done.1 = bf16[1024,1024]{1,0:T(8,128)(2,1)S(1)} copy-done((bf16[1024,1024]{1,0:T(8,128)(2,1)S(1)}, bf16[1024,1024]{1,0:T(8,128)(2,1)}, u32[]{:S(2)}) %copy-start.1) | copy-done | bytes 2097176
  1.6 0.0 copy-start.2
  1.6 0.7 %copy-done.2 = s32[1024,2]{0,1:T(2,128)S(1)} copy-done((s32[1024,2]{0,1:T(2,128)S(1)}, s32[1024,2]{0,1:T(2,128)}, u32[]{:S(2)}) %copy-start.2) | copy-done | bytes 8216
  2.3 0.0 copy-start.3
  2.3 0.7 %copy-done.3 = s32[1024,1]{0,1:T(1,128)S(1)} copy-done((s32[1024,1]{0,1:T(1,128)S(1)}, s32[1024,1]{0,1:T(1,128)}, u32[]{:S(2)}) %copy-start.3) | copy-done | bytes 4120
  3.0 0.0 copy-start.4
  3.0 0.7 %copy-done.4 = f32[2,384]{1,0:T(2,128)S(1)} copy-done((f32[2,384]{1,0:T(2,128)S(1)}, f32[2,384]{1,0:T(2,128)}, u32[]{:S(2)}) %copy-start.4) | copy-done | bytes 3096
  3.7 11.9 %shard_map.64 = (bf16[16,256,128]{2,1,0:T(8,128)(2,1)S(1)}, bf16[16,256,128]{2,1,0:T(8,128)(2,1)S(1)}) custom-call(s32[2,1024]{1,0:T(2,128)S(1)} %bitcast.4, s32[1,1024]{1,0:T(1,128)S(1)} %bitcast.5, f32[2,384]{1,0:T(2,128)S(1)} %copy-done.4, bf16[1024,1024]{1,0:T(8,128)(2,1)S(1)} %copy-done.1, bf16[4,1024,384]{2,1,0:T(8,128)(2,1)} %intens_hbm.1), custom_call_target="tpu_custom_call" | custom-call | tf_op jit(solution)/shard_map/pallas_call | solution.py:327
  15.6 0.1 collective-permute-start
  15.7 2.6 %collective-permute-done = bf16[16,256,128]{2,1,0:T(8,128)(2,1)S(1)} collective-permute-done((bf16[16,256,128]{2,1,0:T(8,128)(2,1)S(1)}, bf16[16,256,128]{2,1,0:T(8,128)(2,1)S(1)}, u32[]{:S(2)}, u32[]{:S(2)}) %collective-permute-start) | collective-permute-done | bytes 1048608 | tf_op jit(solution)/shard_map/ppermute | solution.py:391
  18.4 0.0 copy-start
  18.4 0.3 add_convert_fusion
  18.6 23.6 %all_to_all.10.pieces_ref = bf16[16,256,128]{2,1,0:T(8,128)(2,1)S(1)} all-to-all(bf16[16,256,128]{2,1,0:T(8,128)(2,1)S(1)} %add_convert_fusion), channel_id=1, replica_groups=mesh['z'=8,'xh'=2,'y'=4,'core'=2,'band'=2] {'xh','y','band'}, dimensions={0} | all-to-all | bytes 2097152 | tf_op jit(solution)/shard_map/all_to_all | solution.py:393
  42.3 0.1 shard_map.65
  42.4 16.6 %all_to_all.11.parts_ref = bf16[8,32,128]{2,1,0:T(8,128)(2,1)S(1)} all-to-all(bf16[8,32,128]{2,1,0:T(8,128)(2,1)S(1)} %bitcast.3), channel_id=1, replica_groups=mesh['z'=8,'xh'=2,'y'=4,'core'=2,'band'=2] {'z'}, dimensions={0} | all-to-all | bytes 131072 | tf_op jit(solution)/shard_map/all_to_all | solution.py:397
  59.0 0.0 copy-done
  59.1 1.3 %shard_map.66 = f32[1,4,1024]{2,1,0:T(4,128)} custom-call(bf16[8,32,128]{2,1,0:T(8,128)(2,1)S(1)} %all_to_all.11.parts_ref, bf16[2,1024,1024]{2,1,0:T(8,128)(2,1)S(1)} %copy-done), custom_call_target="tpu_custom_call" | custom-call | tf_op jit(solution)/shard_map/pallas_call | solution.py:380
Async XLA Ops:
  0.0 1.6 %copy-start.1 = (bf16[1024,1024]{1,0:T(8,128)(2,1)S(1)}, bf16[1024,1024]{1,0:T(8,128)(2,1)}, u32[]{:S(2)}) copy-start(bf16[1024,1024]{1,0:T(8,128)(2,1)} %constant.4.clone.table_hbm) | copy-start | bytes 6291460
  1.6 0.7 %copy-start.2 = (s32[1024,2]{0,1:T(2,128)S(1)}, s32[1024,2]{0,1:T(2,128)}, u32[]{:S(2)}) copy-start(s32[1024,2]{0,1:T(2,128)} %param.7) | copy-start | bytes 24580
  2.3 0.7 %copy-start.3 = (s32[1024,1]{0,1:T(1,128)S(1)}, s32[1024,1]{0,1:T(1,128)}, u32[]{:S(2)}) copy-start(s32[1024,1]{0,1:T(1,128)} %param.8) | copy-start | bytes 12292
  3.0 0.7 %copy-start.4 = (f32[2,384]{1,0:T(2,128)S(1)}, f32[2,384]{1,0:T(2,128)}, u32[]{:S(2)}) copy-start(f32[2,384]{1,0:T(2,128)} %gradient_hbm.1) | copy-start | bytes 9220
  15.6 2.7 %collective-permute-start = (bf16[16,256,128]{2,1,0:T(8,128)(2,1)S(1)}, bf16[16,256,128]{2,1,0:T(8,128)(2,1)S(1)}, u32[]{:S(2)}, u32[]{:S(2)}) collective-permute-start(bf16[16,256,128]{2,1,0:T(8,128)(2,1)S(1)} %get-tuple-element.8), channel_id=1, source_target_pairs={{0,2},{2,0},{1,3},{3,1},{4,6},{6,4},{5,7},{7,5},{8,10},{10,8},{9,1... | collective-permute-start | bytes 3145736 | tf_op jit(solution)/shard_map/ppermute | solution.py:391
  18.4 40.7 %copy-start = (bf16[2,1024,1024]{2,1,0:T(8,128)(2,1)S(1)}, bf16[2,1024,1024]{2,1,0:T(8,128)(2,1)}, u32[]{:S(2)}) copy-start(bf16[2,1024,1024]{2,1,0:T(8,128)(2,1)} %constant.5.clone.table_ref) | copy-start | bytes 12582916

commit v3 on v2

v3 whole, which is shorter than its diff:
```python
import math

import jax
import jax.numpy as jnp
import ml_dtypes
import numpy as np
from jax import lax
from jax.experimental import pallas as pl
from jax.experimental.pallas import tpu as pltpu
from jax.sharding import Mesh
from jax.sharding import PartitionSpec as P

NX = 1024
NY = 512
PIX_BLK = 128
BLK_BAND = 3
PIX_BAND = PIX_BLK * BLK_BAND
ROWS_DEV = 4
CAP = 2
HALF_X = NX // 2
CHUNK = 256
STEPS = HALF_X // CHUNK
GROUP = ROWS_DEV * PIX_BLK
DEPTH = BLK_BAND * GROUP
TALL = NY + 16
GRID_Z, GRID_XH, GRID_Y, GRID_CORE, GRID_BAND = 8, 2, 4, 2, 2
PIECES = GRID_XH * GRID_Y * GRID_BAND
ROW_AXES = ("z", "xh", "y", "core")
F32, BF16 = jnp.float32, jnp.bfloat16


def forward_table():
    turns = np.outer(np.arange(HALF_X + 1), np.arange(NX)) % NX
    angle = turns.astype(np.float32) * np.float32(2.0 * math.pi / NX)
    norm_factor = np.float32(1.0 / math.sqrt(NX))
    cosine, sine = np.cos(angle) * norm_factor, np.sin(angle) * norm_factor
    lower = -sine[:HALF_X]
    lower[0] = cosine[HALF_X]
    pieces = np.stack(
        [cosine[:HALF_X].reshape(STEPS, CHUNK, NX), lower.reshape(STEPS, CHUNK, NX)], axis=1
    )
    return pieces.reshape(NX, NX).astype(ml_dtypes.bfloat16)


def backward_table():
    turns = np.outer(np.arange(HALF_X + 1), np.arange(NX)) % NX
    angle = turns.astype(np.float64) * (2.0 * math.pi / NX)
    scale = 1.0 / math.sqrt(NX) / math.sqrt(GRID_BAND * CAP * PIX_BLK)
    upper = np.cos(angle[:HALF_X]) * scale
    upper[0] *= 0.5
    lower = -np.sin(angle[:HALF_X]) * scale
    lower[0] = np.cos(angle[HALF_X]) * scale
    pieces = np.stack(
        [upper.reshape(STEPS, CHUNK, NX), lower.reshape(STEPS, CHUNK, NX)], axis=1
    )
    whole = pieces.reshape(NX, NX).astype(np.float32)
    high = whole.astype(ml_dtypes.bfloat16)
    low = (whole - high.astype(np.float32)).astype(ml_dtypes.bfloat16)
    return np.stack([high, low])


def horner(variable, coefficients):
    total = jnp.full_like(variable, coefficients[-1])
    for coefficient in coefficients[-2::-1]:
        total = total * variable + coefficient
    return total


SINE = [(-1.0) ** k / math.factorial(2 * k + 1) for k in range(8)]
COSINE = [(-1.0) ** k / math.factorial(2 * k) for k in range(8)]


def small_sincos(angle):
    square = angle * angle
    return angle * horner(square, SINE), horner(square, COSINE)


def cycles_sincos(cycles):
    cycles = cycles - jnp.round(cycles)
    sine, cosine = small_sincos(cycles * math.pi)
    return 2.0 * sine * cosine, 1.0 - 2.0 * sine * sine


def own_place():
    z_at, x_high, y_at, core = (lax.axis_index(name) for name in ROW_AXES)
    return ((z_at * GRID_XH + x_high) * GRID_Y + y_at) * GRID_CORE + core, core


def local_kernel(
    facts_ref,
    table_hbm,
    intens_hbm,
    keep_ref,
    send_ref,
    values,
    table_ref,
    shift_base,
    shift_ref,
    coarse_ref,
    fine_ref,
    middle_ref,
    masks_ref,
    rotated,
    products,
    copy_sem,
):
    own_row, own_core = own_place()
    table_copies = []
    for step in range(STEPS):
        rows = pl.ds(step * 2 * CHUNK, 2 * CHUNK)
        table_copies.append(
            pltpu.make_async_copy(table_hbm.at[rows], table_ref.at[rows], copy_sem.at[step])
        )
    block_copies = []
    for block in range(BLK_BAND):
        block_copies.append([])
        for row in range(ROWS_DEV):
            block_copies[block].append(
                pltpu.make_async_copy(
                    intens_hbm.at[row, :, pl.ds(block * PIX_BLK, PIX_BLK)],
                    values.at[:, pl.ds(block * GROUP + row * PIX_BLK, PIX_BLK)],
                    copy_sem.at[STEPS + block * ROWS_DEV + row],
                )
            )
    for copy in table_copies[:1] + sum(block_copies, []) + table_copies[1:]:
        copy.start()

    gradient_x = facts_ref[3:4, 0:PIX_BAND]
    gradient_y = facts_ref[4:5, 0:PIX_BAND]
    eights = lax.broadcasted_iota(jnp.int32, (HALF_X // 8, PIX_BAND), 0).astype(F32)
    coarse_ref[0], coarse_ref[1] = cycles_sincos(gradient_x * (eights * (8.0 / NX)))
    units = lax.broadcasted_iota(jnp.int32, (8, PIX_BAND), 0).astype(F32)
    fine_ref[0], fine_ref[1] = cycles_sincos(gradient_x * (units * (1.0 / NX)))
    middle_ref[0:1, :], middle_ref[1:2, :] = cycles_sincos(gradient_x * 0.5)

    block_ids = lax.broadcasted_iota(jnp.int32, (8, NX), 0).astype(F32)
    counts = facts_ref[2:3, :]
    used = ((facts_ref[0:1, :] == block_ids) & (counts > 0.5)) | (
        (facts_ref[1:2, :] == block_ids) & (counts > 1.5)
    )
    used = used.astype(F32)
    place_sum = lax.broadcasted_iota(jnp.int32, (HALF_X, HALF_X), 0) + lax.broadcasted_iota(
        jnp.int32, (HALF_X, HALF_X), 1
    )
    reverse = (place_sum == HALF_X).astype(F32).astype(BF16)
    mirror = jnp.dot(used[:, HALF_X:].astype(BF16), reverse, preferred_element_type=F32)
    lane_first = lax.broadcasted_iota(jnp.int32, (8, HALF_X), 1) == 0
    ahead = used[:, :HALF_X]
    mirror = jnp.where(lane_first, ahead, mirror)
    for sort, rows in enumerate((ahead + mirror, ahead - mirror)):
        columns = rows.T
        for block in range(BLK_BAND):
            masks_ref[sort * BLK_BAND + block] = jnp.broadcast_to(
                columns[:, block : block + 1], (HALF_X, PIX_BLK)
            ).astype(BF16)

    nearest = jnp.round(gradient_y)
    rest = gradient_y - nearest
    sinc = horner(rest * rest, [SINE[k] * math.pi ** (2 * k) for k in range(8)])
    small = rest * (math.pi / NY)
    peak = sinc * (1.0 - small * small * (1.0 / 3.0))
    parity = nearest - 2.0 * jnp.floor(nearest * 0.5)
    lobes = (1.0 - 2.0 * parity) * (rest * math.pi) * sinc * (1.0 / NY)
    sine_g, cosine_g = small_sincos(gradient_y * (math.pi / NY))
    index = lax.broadcasted_iota(jnp.int32, (TALL, PIX_BLK), 0)
    offset = index - (ROWS_DEV - 1) - ROWS_DEV * own_row
    distance = offset.astype(F32)
    folded = distance - NY * jnp.round(distance * (1.0 / NY))
    sine_d, cosine_d = small_sincos(folded * (math.pi / NY))
    row_sign = (1 - 2 * (offset & 1)).astype(F32)
    first_row = lax.broadcasted_iota(jnp.int32, (TALL - NY, PIX_BLK), 0) == 0

    def shift_block(block):
        lanes = slice(block * PIX_BLK, (block + 1) * PIX_BLK)
        upper = (cosine_d * cosine_g[:, lanes] + sine_d * sine_g[:, lanes]) * row_sign
        lower = sine_d * cosine_g[:, lanes] - cosine_d * sine_g[:, lanes]
        turns = (distance - nearest[:, lanes]) * (1.0 / NY)
        at_peak = turns == jnp.round(turns)
        lower = jnp.where(at_peak, 1.0, lower)
        shift_base[:, lanes] = jnp.where(
            at_peak, peak[:, lanes], -lobes[:, lanes] * upper / lower
        )
        for row in range(ROWS_DEV):
            column = block * GROUP + row * PIX_BLK
            start = ROWS_DEV - 1 - row
            shift_ref[0:NY, column : column + PIX_BLK] = shift_base[
                start : start + NY, lanes
            ].astype(BF16)
            shift_ref[NY:TALL, column : column + PIX_BLK] = jnp.where(
                first_row, lobes[:, lanes] * (1.0 - 2.0 * (row % 2)), 0.0
            ).astype(BF16)

    even = (lax.broadcasted_iota(jnp.int32, (8, 2 * CHUNK), 0) & 1) == 0
    upper_rows = lax.broadcasted_iota(jnp.int32, (8, PIX_BLK), 0) < ROWS_DEV
    first_core = jnp.full((8, PIX_BLK), own_core, jnp.int32) == 0
    contract_last = (((1,), (1,)), ((), ()))
    height = CHUNK // 16

    for step in range(STEPS):
        table_copies[step].wait()
        table = table_ref[step * 2 * CHUNK : (step + 1) * 2 * CHUNK, :]
        for block in range(BLK_BAND):
            lanes = slice(block * PIX_BLK, (block + 1) * PIX_BLK)
            if step == 0:
                for copy in block_copies[block]:
                    copy.wait()
            spectrum = jnp.dot(
                table,
                values[:, block * GROUP : (block + 1) * GROUP],
                preferred_element_type=F32,
            )
            if step == 0:
                shift_block(block)
            spectrum = spectrum.astype(BF16).astype(F32)
            fine_sine, fine_cosine = fine_ref[0, :, lanes], fine_ref[1, :, lanes]
            sines, cosines = [], []
            for octet in range(step * CHUNK // 8, (step + 1) * CHUNK // 8):
                sine_c = coarse_ref[0, octet : octet + 1, lanes]
                cosine_c = coarse_ref[1, octet : octet + 1, lanes]
                sines.append(sine_c * fine_cosine + cosine_c * fine_sine)
                cosines.append(cosine_c * fine_cosine - sine_c * fine_sine)
            sine_p = jnp.concatenate(sines, axis=0)
            cosine_p = jnp.concatenate(cosines, axis=0)
            plus = masks_ref[block, step * CHUNK : (step + 1) * CHUNK]
            minus = masks_ref[BLK_BAND + block, step * CHUNK : (step + 1) * CHUNK]
            for row in range(ROWS_DEV):
                inner = slice(row * PIX_BLK, (row + 1) * PIX_BLK)
                outer = slice(
                    block * GROUP + row * PIX_BLK, block * GROUP + (row + 1) * PIX_BLK
                )
                real_part = spectrum[:CHUNK, inner]
                imag_part = spectrum[CHUNK:, inner]
                turned_real = (real_part * cosine_p + imag_part * sine_p).astype(BF16)
                turned_imag = (imag_part * cosine_p - real_part * sine_p).astype(BF16)
                rotated[0:CHUNK, outer] = turned_real * plus
                rotated[CHUNK : 2 * CHUNK, outer] = turned_imag * plus
                rotated[2 * CHUNK : 3 * CHUNK, outer] = turned_imag * minus
                rotated[3 * CHUNK :, outer] = -turned_real * minus
                if step == 0:
                    only = imag_part[0:1] * used[block : block + 1, HALF_X : HALF_X + 1]
                    top = lax.broadcasted_iota(jnp.int32, (16, PIX_BLK), 0) == 0
                    for start, which in ((CHUNK, 1), (3 * CHUNK, 0)):
                        old = rotated[start : start + 16, outer].astype(F32)
                        rotated[start : start + 16, outer] = jnp.where(
                            top, only * middle_ref[which : which + 1, lanes], old
                        ).astype(BF16)

        products[...] = lax.dot_general(
            shift_ref[...], rotated[...], contract_last, preferred_element_type=F32
        )
        edge_herm = products[NY : NY + 1, : 2 * CHUNK]
        edge_anti = products[NY : NY + 1, 2 * CHUNK :]
        edges = (
            jnp.where(even, -edge_anti, edge_anti),
            jnp.where(even, edge_herm, -edge_herm),
        )
        for x_high in range(GRID_XH):
            for y_at in range(GRID_Y):
                for z_at in range(GRID_Z):
                    start = z_at * 64 + x_high * 32 + y_at * 8
                    for band in range(GRID_BAND):
                        slots = slice(band * 2 * CHUNK, (band + 1) * 2 * CHUNK)
                        whole = products[start : start + 8, slots] + edges[band]
                        kept, sent = [], []
                        for lane in range(0, 2 * CHUNK, 2 * PIX_BLK):
                            left = whole[:, lane : lane + PIX_BLK]
                            right = whole[:, lane + PIX_BLK : lane + 2 * PIX_BLK]
                            low = jnp.where(upper_rows, left, pltpu.roll(right, ROWS_DEV, 0))
                            high = jnp.where(upper_rows, pltpu.roll(left, ROWS_DEV, 0), right)
                            kept.append(jnp.where(first_core, low, high))
                            sent.append(jnp.where(first_core, high, low))
                        piece = (x_high * GRID_Y + y_at) * GRID_BAND + band
                        target = z_at * 32 + step * height
                        where = slice(target, target + height)
                        keep_ref[piece, where, :] = jnp.concatenate(kept, axis=0).astype(BF16)
                        send_ref[piece, where, :] = jnp.concatenate(sent, axis=0).astype(BF16)


VMEM_SPEC = pl.BlockSpec(memory_space=pltpu.VMEM)
HBM_SPEC = pl.BlockSpec(memory_space=pltpu.HBM)
LOCAL_VMEM = 50 * 1024 * 1024


def local_part(facts, table, intens):
    out_shape = jax.ShapeDtypeStruct((PIECES, 32 * GRID_Z, PIX_BLK), BF16)
    return pl.pallas_call(
        local_kernel,
        in_specs=[VMEM_SPEC, HBM_SPEC, HBM_SPEC],
        out_specs=[VMEM_SPEC] * 2,
        out_shape=[out_shape, out_shape],
        scratch_shapes=[
            pltpu.VMEM((NX, DEPTH), BF16),
            pltpu.VMEM((NX, NX), BF16),
            pltpu.VMEM((TALL, PIX_BAND), F32),
            pltpu.VMEM((TALL, DEPTH), BF16),
            pltpu.VMEM((2, HALF_X // 8, PIX_BAND), F32),
            pltpu.VMEM((2, 8, PIX_BAND), F32),
            pltpu.VMEM((2, PIX_BAND), F32),
            pltpu.VMEM((2 * BLK_BAND, HALF_X, PIX_BLK), BF16),
            pltpu.VMEM((4 * CHUNK, DEPTH), BF16),
            pltpu.VMEM((TALL, 4 * CHUNK), F32),
            pltpu.SemaphoreType.DMA((STEPS + BLK_BAND * ROWS_DEV,)),
        ],
        compiler_params=pltpu.CompilerParams(vmem_limit_bytes=LOCAL_VMEM),
    )(facts, table, intens)


def plane_kernel(pieces_ref, plane_ref):
    total = pieces_ref[0].astype(F32)
    for source in range(1, PIECES):
        total = total + pieces_ref[source].astype(F32)
    plane_ref[...] = total.astype(BF16)


def plane_part(pieces):
    return pl.pallas_call(
        plane_kernel,
        in_specs=[VMEM_SPEC],
        out_specs=VMEM_SPEC,
        out_shape=jax.ShapeDtypeStruct((32 * GRID_Z, PIX_BLK), BF16),
        compiler_params=pltpu.CompilerParams(vmem_limit_bytes=32 * 1024 * 1024),
    )(pieces)


def final_kernel(parts_ref, table_ref, image_ref):
    total = parts_ref[0].astype(F32)
    for source in range(1, GRID_Z):
        total = total + parts_ref[source].astype(F32)
    tiles = [total[at : at + ROWS_DEV] for at in range(0, 32, ROWS_DEV)]
    total = jnp.concatenate(tiles, axis=1)
    high = total.astype(BF16)
    low = total - high.astype(F32)
    both = jnp.concatenate([high.astype(F32), low], axis=0).astype(BF16)
    image = jnp.dot(both, table_ref[0], preferred_element_type=F32)
    image = image[:ROWS_DEV] + image[ROWS_DEV:]
    image_ref[0] = image + jnp.dot(high, table_ref[1], preferred_element_type=F32)


def final_part(parts, table):
    return pl.pallas_call(
        final_kernel,
        in_specs=[VMEM_SPEC] * 2,
        out_specs=VMEM_SPEC,
        out_shape=jax.ShapeDtypeStruct((1, ROWS_DEV, NX), F32),
        compiler_params=pltpu.CompilerParams(vmem_limit_bytes=32 * 1024 * 1024),
    )(parts, table)


def body(intens, block_list, block_count, pixel_gradient):
    facts = jnp.concatenate(
        [
            block_list.T.astype(F32),
            block_count.T.astype(F32),
            jnp.pad(pixel_gradient, ((0, 3), (0, NX - PIX_BAND))),
        ],
        axis=0,
    )
    keep, send = local_part(facts, jnp.asarray(forward_table()), intens)
    received = lax.ppermute(send, "core", [(0, 1), (1, 0)])
    chip = (keep.astype(F32) + received.astype(F32)).astype(BF16)
    pieces = lax.all_to_all(
        chip, ("xh", "y", "band"), split_axis=0, concat_axis=0, tiled=True
    )
    plane = plane_part(pieces).reshape(GRID_Z, 32, PIX_BLK)
    parts = lax.all_to_all(plane, "z", split_axis=0, concat_axis=0, tiled=True)
    return final_part(parts, jnp.asarray(backward_table()))


def solution(mesh):
    grid = Mesh(
        mesh.devices.reshape(GRID_Z, GRID_XH, GRID_Y, GRID_CORE, GRID_BAND),
        ROW_AXES + ("band",),
    )
    return jax.shard_map(
        body,
        mesh=grid,
        in_specs=(P(ROW_AXES, None, "band"), P(None, "band"), P(None, "band"), P(None, "band")),
        out_specs=P("band", ROW_AXES, None),
        check_vma=False,
    )
```

time: 60.6 us -> 58.5 us (0.965)
  local copies, waits for them, and re-layouts: 3.66 us -> 0.01 us
  other arithmetic: 0.28 us -> 2.36 us
    unnamed x10 -> x2, local copies, waits for them, and re-layouts: 3.66 us -> 0.01 us
    convert_element_type x0 -> x2, other arithmetic: none -> 1.39 us  [the longest x1 0.7 us: body(): block_list.T.astype(F32)]
    concatenate x0 -> x1, other arithmetic: none -> 0.7 us  [body(): jnp.concatenate([block_list.T.astype(F32), block_count.T.astype(F32), jnp...]
where the time goes in v3:
time: 58.5 us; the launch traced here: 58.2 us
  blocking collectives  40.3 us (69%)
  Pallas kernels  12.8 us (22%)
  waiting for transfers between devices  2.65 us (5%)
  other arithmetic  2.36 us (4%)
    all_to_all x1, blocking collectives, body(): lax.all_to_all(chip, ('xh', 'y', 'band'), split_axis=0, concat_axis=0, ti...  23.6 us
    all_to_all x1, blocking collectives, body(): parts = lax.all_to_all(plane, 'z', split_axis=0, concat_axis=0, tiled=True)  16.6 us
    pallas_call x1, Pallas kernels, local_part(): pl.pallas_call(local_kernel, in_specs=[VMEM_SPEC, HBM_SPEC, HBM_SPEC], ou...  11.4 us
    ppermute x1, waiting for transfers between devices, body(): received = lax.ppermute(send, 'core', [(0, 1), (1, 0)])  2.65 us
    pallas_call x1, Pallas kernels, final_part(): pl.pallas_call(final_kernel, in_specs=[VMEM_SPEC] * 2, out_specs=VMEM_SPE...  1.27 us
  transfers between devices with their start and end apart: 1, of which 1 were waited for; matrix products, arithmetic and copies ran while one was open for 0% of the time, Pallas kernels for 0%

profile of v3, /device:TPU:2, one launch (start us, length us, event | category | flops | bytes accessed | tf_op | source)
XLA Modules:
  0.0 58.2 jit_solution(15497151949786833511)
XLA Ops:
  0.0 0.7 %convert_bitcast_fusion.1 = f32[1,1024]{1,0:T(1,128)S(1)} fusion(s32[1024,1]{0,1:T(1,128)} %param.8), kind=kLoop, calls=%fused_computation.4 | loop fusion | flops 1024 | bytes 8192 | tf_op jit(solution)/shard_map/convert_element_type | solution.py:353
  0.7 0.7 %convert_bitcast_fusion = f32[2,1024]{1,0:T(2,128)S(1)} fusion(s32[1024,2]{0,1:T(2,128)} %param.7), kind=kLoop, calls=%fused_computation.3 | loop fusion | flops 2048 | bytes 16384 | tf_op jit(solution)/shard_map/convert_element_type | solution.py:352
  1.4 0.7 %select_maximum_fusion.facts_ref = f32[8,1024]{1,0:T(8,128)S(1)} fusion(f32[2,384]{1,0:T(2,128)} %param.9, f32[1,1024]{1,0:T(1,128)S(1)} %convert_bitcast_fusion.1, f32[2,1024]{1,0:T(2,128)S(1)} %convert_bitcast_fusion), kind=kLoop, calls=%fused_computation.1 | loop fusion | flops 32768 | bytes 48128 | tf_op jit(solution)/shard_map/concatenate | solution.py:350
  2.1 11.4 %shard_map.64 = (bf16[16,256,128]{2,1,0:T(8,128)(2,1)S(1)}, bf16[16,256,128]{2,1,0:T(8,128)(2,1)S(1)}) custom-call(f32[8,1024]{1,0:T(8,128)S(1)} %select_maximum_fusion.facts_ref, bf16[1024,1024]{1,0:T(8,128)(2,1)} %constant.7.clone.table_hbm, bf16[4,1024,384]{2,1,0:T(8,128)(2,1)} %intens_hbm.1), custom_call_target="tpu_custom_call" | custom-call | tf_op jit(solution)/shard_map/pallas_call | solution.py:286
  13.5 0.1 collective-permute-start
  13.6 2.6 %collective-permute-done = bf16[16,256,128]{2,1,0:T(8,128)(2,1)S(1)} collective-permute-done((bf16[16,256,128]{2,1,0:T(8,128)(2,1)S(1)}, bf16[16,256,128]{2,1,0:T(8,128)(2,1)S(1)}, u32[]{:S(2)}, u32[]{:S(2)}) %collective-permute-start) | collective-permute-done | bytes 1048608 | tf_op jit(solution)/shard_map/ppermute | solution.py:359
  16.2 0.0 copy-start
  16.2 0.3 add_convert_fusion
  16.5 23.6 %all_to_all.10.pieces_ref = bf16[16,256,128]{2,1,0:T(8,128)(2,1)S(1)} all-to-all(bf16[16,256,128]{2,1,0:T(8,128)(2,1)S(1)} %add_convert_fusion), channel_id=1, replica_groups=mesh['z'=8,'xh'=2,'y'=4,'core'=2,'band'=2] {'xh','y','band'}, dimensions={0} | all-to-all | bytes 2097152 | tf_op jit(solution)/shard_map/all_to_all | solution.py:361
  40.2 0.1 shard_map.65
  40.3 16.6 %all_to_all.11.parts_ref = bf16[8,32,128]{2,1,0:T(8,128)(2,1)S(1)} all-to-all(bf16[8,32,128]{2,1,0:T(8,128)(2,1)S(1)} %bitcast.5), channel_id=1, replica_groups=mesh['z'=8,'xh'=2,'y'=4,'core'=2,'band'=2] {'z'}, dimensions={0} | all-to-all | bytes 131072 | tf_op jit(solution)/shard_map/all_to_all | solution.py:365
  56.9 0.0 copy-done
  56.9 1.3 %shard_map.66 = f32[1,4,1024]{2,1,0:T(4,128)} custom-call(bf16[8,32,128]{2,1,0:T(8,128)(2,1)S(1)} %all_to_all.11.parts_ref, bf16[2,1024,1024]{2,1,0:T(8,128)(2,1)S(1)} %copy-done), custom_call_target="tpu_custom_call" | custom-call | tf_op jit(solution)/shard_map/pallas_call | solution.py:340
Async XLA Ops:
  13.5 2.7 %collective-permute-start = (bf16[16,256,128]{2,1,0:T(8,128)(2,1)S(1)}, bf16[16,256,128]{2,1,0:T(8,128)(2,1)S(1)}, u32[]{:S(2)}, u32[]{:S(2)}) collective-permute-start(bf16[16,256,128]{2,1,0:T(8,128)(2,1)S(1)} %get-tuple-element.8), channel_id=1, source_target_pairs={{0,2},{2,0},{1,3},{3,1},{4,6},{6,4},{5,7},{7,5},{8,10},{10,8},{9,1... | collective-permute-start | bytes 3145736 | tf_op jit(solution)/shard_map/ppermute | solution.py:359
  16.2 40.7 %copy-start = (bf16[2,1024,1024]{2,1,0:T(8,128)(2,1)S(1)}, bf16[2,1024,1024]{2,1,0:T(8,128)(2,1)}, u32[]{:S(2)}) copy-start(bf16[2,1024,1024]{2,1,0:T(8,128)(2,1)} %constant.8.clone.table_ref) | copy-start | bytes 12582916

commit v4 on v3

v4 whole, which is shorter than its diff:
```python
import math

import jax
import jax.numpy as jnp
import ml_dtypes
import numpy as np
from jax import lax
from jax.experimental import pallas as pl
from jax.experimental.pallas import tpu as pltpu
from jax.sharding import Mesh
from jax.sharding import PartitionSpec as P

NX = 1024
NY = 512
PIX_BLK = 128
BLK_BAND = 3
PIX_BAND = PIX_BLK * BLK_BAND
ROWS_DEV = 4
CAP = 2
HALF_X = NX // 2
CHUNK = 256
STEPS = HALF_X // CHUNK
GROUP = ROWS_DEV * PIX_BLK
DEPTH = BLK_BAND * GROUP
TALL = NY + 16
GRID_Z, GRID_XH, GRID_Y, GRID_CORE, GRID_BAND = 8, 2, 4, 2, 2
PIECES = GRID_XH * GRID_Y * GRID_BAND
ROW_AXES = ("z", "xh", "y", "core")
F32, BF16 = jnp.float32, jnp.bfloat16


def forward_table():
    turns = np.outer(np.arange(HALF_X + 1), np.arange(NX)) % NX
    angle = turns.astype(np.float32) * np.float32(2.0 * math.pi / NX)
    norm_factor = np.float32(1.0 / math.sqrt(NX))
    cosine, sine = np.cos(angle) * norm_factor, np.sin(angle) * norm_factor
    lower = -sine[:HALF_X]
    lower[0] = cosine[HALF_X]
    pieces = np.stack(
        [cosine[:HALF_X].reshape(STEPS, CHUNK, NX), lower.reshape(STEPS, CHUNK, NX)], axis=1
    )
    return pieces.reshape(NX, NX).astype(ml_dtypes.bfloat16)


def backward_table():
    turns = np.outer(np.arange(HALF_X + 1), np.arange(NX)) % NX
    angle = turns.astype(np.float64) * (2.0 * math.pi / NX)
    scale = 1.0 / math.sqrt(NX) / math.sqrt(GRID_BAND * CAP * PIX_BLK)
    upper = np.cos(angle[:HALF_X]) * scale
    upper[0] *= 0.5
    lower = -np.sin(angle[:HALF_X]) * scale
    lower[0] = np.cos(angle[HALF_X]) * scale
    pieces = np.stack(
        [upper.reshape(STEPS, CHUNK, NX), lower.reshape(STEPS, CHUNK, NX)], axis=1
    )
    whole = pieces.reshape(NX, NX).astype(np.float32)
    high = whole.astype(ml_dtypes.bfloat16)
    low = (whole - high.astype(np.float32)).astype(ml_dtypes.bfloat16)
    return np.stack([high, low])


def horner(variable, coefficients):
    total = jnp.full_like(variable, coefficients[-1])
    for coefficient in coefficients[-2::-1]:
        total = total * variable + coefficient
    return total


SINE = [(-1.0) ** k / math.factorial(2 * k + 1) for k in range(8)]
COSINE = [(-1.0) ** k / math.factorial(2 * k) for k in range(8)]


def small_sincos(angle):
    square = angle * angle
    return angle * horner(square, SINE), horner(square, COSINE)


def cycles_sincos(cycles):
    cycles = cycles - jnp.round(cycles)
    sine, cosine = small_sincos(cycles * math.pi)
    return 2.0 * sine * cosine, 1.0 - 2.0 * sine * sine


def own_place():
    z_at, x_high, y_at, core = (lax.axis_index(name) for name in ROW_AXES)
    return ((z_at * GRID_XH + x_high) * GRID_Y + y_at) * GRID_CORE + core, core


def local_kernel(
    lists_hbm,
    counts_hbm,
    gradient_hbm,
    table_hbm,
    intens_hbm,
    keep_ref,
    send_ref,
    lists_ref,
    counts_ref,
    gradient_ref,
    values,
    table_ref,
    shift_base,
    shift_ref,
    coarse_ref,
    fine_ref,
    middle_ref,
    masks_ref,
    middle_used,
    rotated,
    products,
    copy_sem,
):
    own_row, own_core = own_place()
    small_copies = [
        pltpu.make_async_copy(gradient_hbm, gradient_ref, copy_sem.at[0]),
        pltpu.make_async_copy(lists_hbm, lists_ref, copy_sem.at[1]),
        pltpu.make_async_copy(counts_hbm, counts_ref, copy_sem.at[2]),
    ]
    table_copies = []
    for step in range(STEPS):
        rows = pl.ds(step * 2 * CHUNK, 2 * CHUNK)
        table_copies.append(
            pltpu.make_async_copy(table_hbm.at[rows], table_ref.at[rows], copy_sem.at[3 + step])
        )
    block_copies = []
    for block in range(BLK_BAND):
        block_copies.append([])
        for row in range(ROWS_DEV):
            block_copies[block].append(
                pltpu.make_async_copy(
                    intens_hbm.at[row, :, pl.ds(block * PIX_BLK, PIX_BLK)],
                    values.at[:, pl.ds(block * GROUP + row * PIX_BLK, PIX_BLK)],
                    copy_sem.at[3 + STEPS + block * ROWS_DEV + row],
                )
            )
    for copy in small_copies + table_copies[:1] + sum(block_copies, []) + table_copies[1:]:
        copy.start()
    for copy in small_copies:
        copy.wait()

    gradient_x = gradient_ref[0:1, :]
    gradient_y = gradient_ref[1:2, :]
    eights = lax.broadcasted_iota(jnp.int32, (HALF_X // 8, PIX_BAND), 0).astype(F32)
    coarse_ref[0], coarse_ref[1] = cycles_sincos(gradient_x * (eights * (8.0 / NX)))
    units = lax.broadcasted_iota(jnp.int32, (8, PIX_BAND), 0).astype(F32)
    fine_ref[0], fine_ref[1] = cycles_sincos(gradient_x * (units * (1.0 / NX)))
    middle_ref[0:1, :], middle_ref[1:2, :] = cycles_sincos(gradient_x * 0.5)

    def make_masks():
        block_ids = lax.broadcasted_iota(jnp.int32, (8, NX), 0)
        counts = counts_ref[0:1, :]
        used = ((lists_ref[0:1, :] == block_ids) & (counts > 0)) | (
            (lists_ref[1:2, :] == block_ids) & (counts > 1)
        )
        used = used.astype(F32)
        place_sum = lax.broadcasted_iota(
            jnp.int32, (HALF_X, HALF_X), 0
        ) + lax.broadcasted_iota(jnp.int32, (HALF_X, HALF_X), 1)
        reverse = (place_sum == HALF_X).astype(F32).astype(BF16)
        mirror = jnp.dot(
            used[:, HALF_X:].astype(BF16), reverse, preferred_element_type=F32
        )
        lane_first = lax.broadcasted_iota(jnp.int32, (8, HALF_X), 1) == 0
        ahead = used[:, :HALF_X]
        mirror = jnp.where(lane_first, ahead, mirror)
        for sort, rows in enumerate((ahead + mirror, ahead - mirror)):
            columns = rows.T
            for block in range(BLK_BAND):
                masks_ref[sort * BLK_BAND + block] = jnp.broadcast_to(
                    columns[:, block : block + 1], (HALF_X, PIX_BLK)
                ).astype(BF16)
        middle_used[...] = jnp.broadcast_to(used[:, HALF_X : HALF_X + 1], (8, PIX_BLK))

    def shift_block(block):
        lanes = slice(block * PIX_BLK, (block + 1) * PIX_BLK)
        gradient = gradient_y[:, lanes]
        nearest = jnp.round(gradient)
        rest = gradient - nearest
        sinc = horner(rest * rest, [SINE[k] * math.pi ** (2 * k) for k in range(8)])
        small = rest * (math.pi / NY)
        peak = sinc * (1.0 - small * small * (1.0 / 3.0))
        parity = nearest - 2.0 * jnp.floor(nearest * 0.5)
        lobes = (1.0 - 2.0 * parity) * (rest * math.pi) * sinc * (1.0 / NY)
        sine_g, cosine_g = small_sincos(gradient * (math.pi / NY))
        index = lax.broadcasted_iota(jnp.int32, (TALL, PIX_BLK), 0)
        offset = index - (ROWS_DEV - 1) - ROWS_DEV * own_row
        distance = offset.astype(F32)
        folded = distance - NY * jnp.round(distance * (1.0 / NY))
        sine_d, cosine_d = small_sincos(folded * (math.pi / NY))
        row_sign = (1 - 2 * (offset & 1)).astype(F32)
        first_row = lax.broadcasted_iota(jnp.int32, (TALL - NY, PIX_BLK), 0) == 0
        upper = (cosine_d * cosine_g + sine_d * sine_g) * row_sign
        lower = sine_d * cosine_g - cosine_d * sine_g
        turns = (distance - nearest) * (1.0 / NY)
        at_peak = turns == jnp.round(turns)
        lower = jnp.where(at_peak, 1.0, lower)
        shift_base[:, lanes] = jnp.where(at_peak, peak, -lobes * upper / lower)
        for row in range(ROWS_DEV):
            column = block * GROUP + row * PIX_BLK
            start = ROWS_DEV - 1 - row
            shift_ref[0:NY, column : column + PIX_BLK] = shift_base[
                start : start + NY, lanes
            ].astype(BF16)
            shift_ref[NY:TALL, column : column + PIX_BLK] = jnp.where(
                first_row, lobes * (1.0 - 2.0 * (row % 2)), 0.0
            ).astype(BF16)

    def transform(step, block):
        return jnp.dot(
            table_ref[step * 2 * CHUNK : (step + 1) * 2 * CHUNK, :],
            values[:, block * GROUP : (block + 1) * GROUP],
            preferred_element_type=F32,
        )

    def rotate(step, block, spectrum):
        lanes = slice(block * PIX_BLK, (block + 1) * PIX_BLK)
        spectrum = spectrum.astype(BF16).astype(F32)
        fine_sine, fine_cosine = fine_ref[0, :, lanes], fine_ref[1, :, lanes]
        sines, cosines = [], []
        for octet in range(step * CHUNK // 8, (step + 1) * CHUNK // 8):
            sine_c = coarse_ref[0, octet : octet + 1, lanes]
            cosine_c = coarse_ref[1, octet : octet + 1, lanes]
            sines.append(sine_c * fine_cosine + cosine_c * fine_sine)
            cosines.append(cosine_c * fine_cosine - sine_c * fine_sine)
        sine_p = jnp.concatenate(sines, axis=0)
        cosine_p = jnp.concatenate(cosines, axis=0)
        plus = masks_ref[block, step * CHUNK : (step + 1) * CHUNK]
        minus = masks_ref[BLK_BAND + block, step * CHUNK : (step + 1) * CHUNK]
        for row in range(ROWS_DEV):
            inner = slice(row * PIX_BLK, (row + 1) * PIX_BLK)
            outer = slice(block * GROUP + row * PIX_BLK, block * GROUP + (row + 1) * PIX_BLK)
            real_part = spectrum[:CHUNK, inner]
            imag_part = spectrum[CHUNK:, inner]
            turned_real = (real_part * cosine_p + imag_part * sine_p).astype(BF16)
            turned_imag = (imag_part * cosine_p - real_part * sine_p).astype(BF16)
            rotated[step, 0:CHUNK, outer] = turned_real * plus
            rotated[step, CHUNK : 2 * CHUNK, outer] = turned_imag * plus
            rotated[step, 2 * CHUNK : 3 * CHUNK, outer] = turned_imag * minus
            rotated[step, 3 * CHUNK :, outer] = -turned_real * minus
            if step == 0:
                only = imag_part[0:1] * middle_used[block : block + 1, :]
                top = lax.broadcasted_iota(jnp.int32, (16, PIX_BLK), 0) == 0
                for start, which in ((CHUNK, 1), (3 * CHUNK, 0)):
                    old = rotated[step, start : start + 16, outer].astype(F32)
                    rotated[step, start : start + 16, outer] = jnp.where(
                        top, only * middle_ref[which : which + 1, lanes], old
                    ).astype(BF16)

    def multiply(step, rows):
        products[step, rows, :] = lax.dot_general(
            shift_ref[rows, :],
            rotated[step],
            (((1,), (1,)), ((), ())),
            preferred_element_type=F32,
        )

    even = (lax.broadcasted_iota(jnp.int32, (8, 2 * CHUNK), 0) & 1) == 0
    upper_rows = lax.broadcasted_iota(jnp.int32, (8, PIX_BLK), 0) < ROWS_DEV
    first_core = jnp.full((8, PIX_BLK), own_core, jnp.int32) == 0
    height = CHUNK // 16

    def store(step, z_range):
        edge_herm = products[step, NY : NY + 1, : 2 * CHUNK]
        edge_anti = products[step, NY : NY + 1, 2 * CHUNK :]
        edges = (
            jnp.where(even, -edge_anti, edge_anti),
            jnp.where(even, edge_herm, -edge_herm),
        )
        for z_at in z_range:
            for x_high in range(GRID_XH):
                for y_at in range(GRID_Y):
                    start = z_at * 64 + x_high * 32 + y_at * 8
                    for band in range(GRID_BAND):
                        slots = slice(band * 2 * CHUNK, (band + 1) * 2 * CHUNK)
                        whole = products[step, start : start + 8, slots] + edges[band]
                        kept, sent = [], []
                        for lane in range(0, 2 * CHUNK, 2 * PIX_BLK):
                            left = whole[:, lane : lane + PIX_BLK]
                            right = whole[:, lane + PIX_BLK : lane + 2 * PIX_BLK]
                            low = jnp.where(upper_rows, left, pltpu.roll(right, ROWS_DEV, 0))
                            high = jnp.where(upper_rows, pltpu.roll(left, ROWS_DEV, 0), right)
                            kept.append(jnp.where(first_core, low, high))
                            sent.append(jnp.where(first_core, high, low))
                        piece = (x_high * GRID_Y + y_at) * GRID_BAND + band
                        target = z_at * 32 + step * height
                        where = slice(target, target + height)
                        keep_ref[piece, where, :] = jnp.concatenate(kept, axis=0)
                        send_ref[piece, where, :] = jnp.concatenate(sent, axis=0).astype(BF16)

    def wait_for(copies):
        for copy in copies:
            copy.wait()

    wait_for(table_copies[:1] + block_copies[0])
    spectrum = transform(0, 0)
    make_masks()
    rotate(0, 0, spectrum)
    wait_for(block_copies[1])
    spectrum = transform(0, 1)
    shift_block(0)
    rotate(0, 1, spectrum)
    wait_for(block_copies[2] + table_copies[1:])
    spectrum = transform(0, 2)
    shift_block(1)
    rotate(0, 2, spectrum)
    spectrum = transform(1, 0)
    shift_block(2)
    rotate(1, 0, spectrum)
    spectrum = transform(1, 1)
    rotate(1, 1, spectrum)
    spectrum = transform(1, 2)
    multiply(0, slice(NY // 2, TALL))
    rotate(1, 2, spectrum)
    multiply(0, slice(0, NY // 2))
    store(0, range(GRID_Z // 2, GRID_Z))
    multiply(1, slice(NY // 2, TALL))
    store(0, range(GRID_Z // 2))
    multiply(1, slice(0, NY // 2))
    store(1, range(GRID_Z // 2, GRID_Z))
    store(1, range(GRID_Z // 2))


VMEM_SPEC = pl.BlockSpec(memory_space=pltpu.VMEM)
HBM_SPEC = pl.BlockSpec(memory_space=pltpu.HBM)
LOCAL_VMEM = 50 * 1024 * 1024


def local_part(lists, counts, gradient, table, intens):
    shape = (PIECES, 32 * GRID_Z, PIX_BLK)
    return pl.pallas_call(
        local_kernel,
        in_specs=[HBM_SPEC] * 5,
        out_specs=[VMEM_SPEC] * 2,
        out_shape=[jax.ShapeDtypeStruct(shape, F32), jax.ShapeDtypeStruct(shape, BF16)],
        scratch_shapes=[
            pltpu.VMEM((CAP, NX), jnp.int32),
            pltpu.VMEM((1, NX), jnp.int32),
            pltpu.VMEM((2, PIX_BAND), F32),
            pltpu.VMEM((NX, DEPTH), BF16),
            pltpu.VMEM((NX, NX), BF16),
            pltpu.VMEM((TALL, PIX_BAND), F32),
            pltpu.VMEM((TALL, DEPTH), BF16),
            pltpu.VMEM((2, HALF_X // 8, PIX_BAND), F32),
            pltpu.VMEM((2, 8, PIX_BAND), F32),
            pltpu.VMEM((2, PIX_BAND), F32),
            pltpu.VMEM((2 * BLK_BAND, HALF_X, PIX_BLK), BF16),
            pltpu.VMEM((8, PIX_BLK), F32),
            pltpu.VMEM((STEPS, 4 * CHUNK, DEPTH), BF16),
            pltpu.VMEM((STEPS, TALL, 4 * CHUNK), F32),
            pltpu.SemaphoreType.DMA((3 + STEPS + BLK_BAND * ROWS_DEV,)),
        ],
        compiler_params=pltpu.CompilerParams(vmem_limit_bytes=LOCAL_VMEM),
    )(lists, counts, gradient, table, intens)


def plane_kernel(pieces_ref, plane_ref):
    total = pieces_ref[0].astype(F32)
    for source in range(1, PIECES):
        total = total + pieces_ref[source].astype(F32)
    plane_ref[...] = total.astype(BF16)


def plane_part(pieces):
    return pl.pallas_call(
        plane_kernel,
        in_specs=[VMEM_SPEC],
        out_specs=VMEM_SPEC,
        out_shape=jax.ShapeDtypeStruct((32 * GRID_Z, PIX_BLK), BF16),
        compiler_params=pltpu.CompilerParams(vmem_limit_bytes=32 * 1024 * 1024),
    )(pieces)


def final_kernel(parts_ref, table_ref, image_ref):
    total = parts_ref[0].astype(F32)
    for source in range(1, GRID_Z):
        total = total + parts_ref[source].astype(F32)
    tiles = [total[at : at + ROWS_DEV] for at in range(0, 32, ROWS_DEV)]
    total = jnp.concatenate(tiles, axis=1)
    high = total.astype(BF16)
    low = total - high.astype(F32)
    both = jnp.concatenate([high.astype(F32), low], axis=0).astype(BF16)
    image = jnp.dot(both, table_ref[0], preferred_element_type=F32)
    image = image[:ROWS_DEV] + image[ROWS_DEV:]
    image_ref[0] = image + jnp.dot(high, table_ref[1], preferred_element_type=F32)


def final_part(parts, table):
    return pl.pallas_call(
        final_kernel,
        in_specs=[VMEM_SPEC] * 2,
        out_specs=VMEM_SPEC,
        out_shape=jax.ShapeDtypeStruct((1, ROWS_DEV, NX), F32),
        compiler_params=pltpu.CompilerParams(vmem_limit_bytes=32 * 1024 * 1024),
    )(parts, table)


def body(intens, block_list, block_count, pixel_gradient):
    keep, send = local_part(
        block_list.T, block_count.T, pixel_gradient, jnp.asarray(forward_table()), intens
    )
    received = lax.ppermute(send, "core", [(0, 1), (1, 0)])
    chip = (keep + received.astype(F32)).astype(BF16)
    pieces = lax.all_to_all(
        chip, ("xh", "y", "band"), split_axis=0, concat_axis=0, tiled=True
    )
    plane = plane_part(pieces).reshape(GRID_Z, 32, PIX_BLK)
    parts = lax.all_to_all(plane, "z", split_axis=0, concat_axis=0, tiled=True)
    return final_part(parts, jnp.asarray(backward_table()))


def solution(mesh):
    grid = Mesh(
        mesh.devices.reshape(GRID_Z, GRID_XH, GRID_Y, GRID_CORE, GRID_BAND),
        ROW_AXES + ("band",),
    )
    return jax.shard_map(
        body,
        mesh=grid,
        in_specs=(P(ROW_AXES, None, "band"), P(None, "band"), P(None, "band"), P(None, "band")),
        out_specs=P("band", ROW_AXES, None),
        check_vma=False,
    )
```

time: 58.5 us -> 59 us (level)
  other arithmetic: 2.36 us -> 0.3 us
  local copies, waits for them, and re-layouts: 0.01 us -> 2.07 us
    unnamed x2 -> x8, local copies, waits for them, and re-layouts: 0.01 us -> 2.07 us
    convert_element_type x3 -> x1, other arithmetic: 1.67 us -> 0.3 us  [body(): chip = (keep + received.astype(F32)).astype(BF16)]
    concatenate x1 -> x0, other arithmetic: 0.7 us -> none  [body(): jnp.concatenate([block_list.T.astype(F32), block_count.T.astype(F32), jnp...]
where the time goes in v4:
time: 59 us; the launch traced here: 58.7 us
  blocking collectives  40.3 us (68%)
  Pallas kernels  13.3 us (23%)
  waiting for transfers between devices  2.65 us (4%)
  local copies, waits for them, and re-layouts  2.07 us (4%)
    all_to_all x1, blocking collectives, body(): lax.all_to_all(chip, ('xh', 'y', 'band'), split_axis=0, concat_axis=0, ti...  23.6 us
    all_to_all x1, blocking collectives, body(): parts = lax.all_to_all(plane, 'z', split_axis=0, concat_axis=0, tiled=True)  16.6 us
    pallas_call x1, Pallas kernels, local_part(): pl.pallas_call(local_kernel, in_specs=[HBM_SPEC] * 5, out_specs=[VMEM_SPE...  11.9 us
    ppermute x1, waiting for transfers between devices, body(): received = lax.ppermute(send, 'core', [(0, 1), (1, 0)])  2.65 us
    unnamed x8, local copies, waits for them, and re-layouts  2.07 us
    pallas_call x1, Pallas kernels, final_part(): pl.pallas_call(final_kernel, in_specs=[VMEM_SPEC] * 2, out_specs=VMEM_SPE...  1.27 us
  transfers between devices with their start and end apart: 1, of which 1 were waited for; matrix products, arithmetic and copies ran while one was open for 0% of the time, Pallas kernels for 0%

profile of v4, /device:TPU:2, one launch (start us, length us, event | category | flops | bytes accessed | tf_op | source)
XLA Modules:
  0.0 58.7 jit_solution(9451664275917092647)
XLA Ops:
  0.0 0.0 copy-start.1
  0.0 0.7 %copy-done.1 = s32[1024,2]{0,1:T(2,128)S(1)} copy-done((s32[1024,2]{0,1:T(2,128)S(1)}, s32[1024,2]{0,1:T(2,128)}, u32[]{:S(2)}) %copy-start.1) | copy-done | bytes 8216
  0.7 0.0 copy-start.2
  0.7 0.7 %copy-done.2 = s32[1024,1]{0,1:T(1,128)S(1)} copy-done((s32[1024,1]{0,1:T(1,128)S(1)}, s32[1024,1]{0,1:T(1,128)}, u32[]{:S(2)}) %copy-start.2) | copy-done | bytes 4120
  1.4 0.0 copy-start.3
  1.4 0.7 %copy-done.3 = f32[2,384]{1,0:T(2,128)S(1)} copy-done((f32[2,384]{1,0:T(2,128)S(1)}, f32[2,384]{1,0:T(2,128)}, u32[]{:S(2)}) %copy-start.3) | copy-done | bytes 3096
  2.1 11.9 %shard_map.64 = (f32[16,256,128]{2,1,0:T(8,128)S(1)}, bf16[16,256,128]{2,1,0:T(8,128)(2,1)S(1)}) custom-call(s32[2,1024]{1,0:T(2,128)S(1)} %bitcast.4, s32[1,1024]{1,0:T(1,128)S(1)} %bitcast.5, f32[2,384]{1,0:T(2,128)S(1)} %copy-done.3, bf16[1024,1024]{1,0:T(8,128)(2,1)} %constant.4.clone.table_hbm, bf16[4,1024,384]{2,1,0:T(8,128)(2,1)} %intens_hbm.1), custom_call_target="tpu_custom_call" | custom-call | tf_op jit(solution)/shard_map/pallas_call | solution.py:330
  14.0 0.1 collective-permute-start
  14.1 2.6 %collective-permute-done = bf16[16,256,128]{2,1,0:T(8,128)(2,1)S(1)} collective-permute-done((bf16[16,256,128]{2,1,0:T(8,128)(2,1)S(1)}, bf16[16,256,128]{2,1,0:T(8,128)(2,1)S(1)}, u32[]{:S(2)}, u32[]{:S(2)}) %collective-permute-start) | collective-permute-done | bytes 1048608 | tf_op jit(solution)/shard_map/ppermute | solution.py:401
  16.7 0.0 copy-start
  16.7 0.3 add_convert_fusion
  17.0 23.6 %all_to_all.10.pieces_ref = bf16[16,256,128]{2,1,0:T(8,128)(2,1)S(1)} all-to-all(bf16[16,256,128]{2,1,0:T(8,128)(2,1)S(1)} %add_convert_fusion), channel_id=1, replica_groups=mesh['z'=8,'xh'=2,'y'=4,'core'=2,'band'=2] {'xh','y','band'}, dimensions={0} | all-to-all | bytes 2097152 | tf_op jit(solution)/shard_map/all_to_all | solution.py:403
  40.7 0.1 shard_map.65
  40.8 16.6 %all_to_all.11.parts_ref = bf16[8,32,128]{2,1,0:T(8,128)(2,1)S(1)} all-to-all(bf16[8,32,128]{2,1,0:T(8,128)(2,1)S(1)} %bitcast.3), channel_id=1, replica_groups=mesh['z'=8,'xh'=2,'y'=4,'core'=2,'band'=2] {'z'}, dimensions={0} | all-to-all | bytes 131072 | tf_op jit(solution)/shard_map/all_to_all | solution.py:407
  57.4 0.0 copy-done
  57.4 1.3 %shard_map.66 = f32[1,4,1024]{2,1,0:T(4,128)} custom-call(bf16[8,32,128]{2,1,0:T(8,128)(2,1)S(1)} %all_to_all.11.parts_ref, bf16[2,1024,1024]{2,1,0:T(8,128)(2,1)S(1)} %copy-done), custom_call_target="tpu_custom_call" | custom-call | tf_op jit(solution)/shard_map/pallas_call | solution.py:388
Async XLA Ops:
  0.0 0.7 %copy-start.1 = (s32[1024,2]{0,1:T(2,128)S(1)}, s32[1024,2]{0,1:T(2,128)}, u32[]{:S(2)}) copy-start(s32[1024,2]{0,1:T(2,128)} %param.7) | copy-start | bytes 24580
  0.7 0.7 %copy-start.2 = (s32[1024,1]{0,1:T(1,128)S(1)}, s32[1024,1]{0,1:T(1,128)}, u32[]{:S(2)}) copy-start(s32[1024,1]{0,1:T(1,128)} %param.8) | copy-start | bytes 12292
  1.4 0.7 %copy-start.3 = (f32[2,384]{1,0:T(2,128)S(1)}, f32[2,384]{1,0:T(2,128)}, u32[]{:S(2)}) copy-start(f32[2,384]{1,0:T(2,128)} %gradient_hbm.1) | copy-start | bytes 9220
  14.0 2.7 %collective-permute-start = (bf16[16,256,128]{2,1,0:T(8,128)(2,1)S(1)}, bf16[16,256,128]{2,1,0:T(8,128)(2,1)S(1)}, u32[]{:S(2)}, u32[]{:S(2)}) collective-permute-start(bf16[16,256,128]{2,1,0:T(8,128)(2,1)S(1)} %get-tuple-element.8), channel_id=1, source_target_pairs={{0,2},{2,0},{1,3},{3,1},{4,6},{6,4},{5,7},{7,5},{8,10},{10,8},{9,1... | collective-permute-start | bytes 3145736 | tf_op jit(solution)/shard_map/ppermute | solution.py:401
  16.7 40.7 %copy-start = (bf16[2,1024,1024]{2,1,0:T(8,128)(2,1)S(1)}, bf16[2,1024,1024]{2,1,0:T(8,128)(2,1)}, u32[]{:S(2)}) copy-start(bf16[2,1024,1024]{2,1,0:T(8,128)(2,1)} %constant.5.clone.table_ref) | copy-start | bytes 12582916

commit v5 on v4

--- a/solution.py
+++ b/solution.py
@@ -87,16 +87,11 @@
 
 
 def local_kernel(
-    lists_hbm,
-    counts_hbm,
-    gradient_hbm,
+    facts_ref,
     table_hbm,
     intens_hbm,
     keep_ref,
     send_ref,
-    lists_ref,
-    counts_ref,
-    gradient_ref,
     values,
     table_ref,
     shift_base,
@@ -111,16 +106,11 @@
     copy_sem,
 ):
     own_row, own_core = own_place()
-    small_copies = [
-        pltpu.make_async_copy(gradient_hbm, gradient_ref, copy_sem.at[0]),
-        pltpu.make_async_copy(lists_hbm, lists_ref, copy_sem.at[1]),
-        pltpu.make_async_copy(counts_hbm, counts_ref, copy_sem.at[2]),
-    ]
     table_copies = []
     for step in range(STEPS):
         rows = pl.ds(step * 2 * CHUNK, 2 * CHUNK)
         table_copies.append(
-            pltpu.make_async_copy(table_hbm.at[rows], table_ref.at[rows], copy_sem.at[3 + step])
+            pltpu.make_async_copy(table_hbm.at[rows], table_ref.at[rows], copy_sem.at[step])
         )
     block_copies = []
     for block in range(BLK_BAND):
@@ -130,16 +120,14 @@
                 pltpu.make_async_copy(
                     intens_hbm.at[row, :, pl.ds(block * PIX_BLK, PIX_BLK)],
                     values.at[:, pl.ds(block * GROUP + row * PIX_BLK, PIX_BLK)],
-                    copy_sem.at[3 + STEPS + block * ROWS_DEV + row],
+                    copy_sem.at[STEPS + block * ROWS_DEV + row],
                 )
             )
-    for copy in small_copies + table_copies[:1] + sum(block_copies, []) + table_copies[1:]:
+    for copy in table_copies[:1] + sum(block_copies, []) + table_copies[1:]:
         copy.start()
-    for copy in small_copies:
-        copy.wait()
-
-    gradient_x = gradient_ref[0:1, :]
-    gradient_y = gradient_ref[1:2, :]
+
+    gradient_x = facts_ref[1:2, 0:PIX_BAND]
+    gradient_y = facts_ref[2:3, 0:PIX_BAND]
     eights = lax.broadcasted_iota(jnp.int32, (HALF_X // 8, PIX_BAND), 0).astype(F32)
     coarse_ref[0], coarse_ref[1] = cycles_sincos(gradient_x * (eights * (8.0 / NX)))
     units = lax.broadcasted_iota(jnp.int32, (8, PIX_BAND), 0).astype(F32)
@@ -148,9 +136,10 @@
 
     def make_masks():
         block_ids = lax.broadcasted_iota(jnp.int32, (8, NX), 0)
-        counts = counts_ref[0:1, :]
-        used = ((lists_ref[0:1, :] == block_ids) & (counts > 0)) | (
-            (lists_ref[1:2, :] == block_ids) & (counts > 1)
+        packed = facts_ref[0:1, :].astype(jnp.int32)
+        counts = packed >> 4
+        used = (((packed & 3) == block_ids) & (counts > 0)) | (
+            (((packed >> 2) & 3) == block_ids) & (counts > 1)
         )
         used = used.astype(F32)
         place_sum = lax.broadcasted_iota(
@@ -170,6 +159,8 @@
                     columns[:, block : block + 1], (HALF_X, PIX_BLK)
                 ).astype(BF16)
         middle_used[...] = jnp.broadcast_to(used[:, HALF_X : HALF_X + 1], (8, PIX_BLK))
+
+    upper_rows = lax.broadcasted_iota(jnp.int32, (8, PIX_BLK), 0) < ROWS_DEV
 
     def shift_block(block):
         lanes = slice(block * PIX_BLK, (block + 1) * PIX_BLK)
@@ -182,28 +173,50 @@
         parity = nearest - 2.0 * jnp.floor(nearest * 0.5)
         lobes = (1.0 - 2.0 * parity) * (rest * math.pi) * sinc * (1.0 / NY)
         sine_g, cosine_g = small_sincos(gradient * (math.pi / NY))
-        index = lax.broadcasted_iota(jnp.int32, (TALL, PIX_BLK), 0)
-        offset = index - (ROWS_DEV - 1) - ROWS_DEV * own_row
-        distance = offset.astype(F32)
-        folded = distance - NY * jnp.round(distance * (1.0 / NY))
-        sine_d, cosine_d = small_sincos(folded * (math.pi / NY))
-        row_sign = (1 - 2 * (offset & 1)).astype(F32)
         first_row = lax.broadcasted_iota(jnp.int32, (TALL - NY, PIX_BLK), 0) == 0
-        upper = (cosine_d * cosine_g + sine_d * sine_g) * row_sign
-        lower = sine_d * cosine_g - cosine_d * sine_g
-        turns = (distance - nearest) * (1.0 / NY)
-        at_peak = turns == jnp.round(turns)
-        lower = jnp.where(at_peak, 1.0, lower)
-        shift_base[:, lanes] = jnp.where(at_peak, peak, -lobes * upper / lower)
         for row in range(ROWS_DEV):
             column = block * GROUP + row * PIX_BLK
-            start = ROWS_DEV - 1 - row
-            shift_ref[0:NY, column : column + PIX_BLK] = shift_base[
-                start : start + NY, lanes
-            ].astype(BF16)
             shift_ref[NY:TALL, column : column + PIX_BLK] = jnp.where(
                 first_row, lobes * (1.0 - 2.0 * (row % 2)), 0.0
             ).astype(BF16)
+        for half in range(GRID_CORE):
+            core = own_core if half == 0 else 1 - own_core
+            offset = (
+                lax.broadcasted_iota(jnp.int32, (NY, PIX_BLK), 0)
+                - (ROWS_DEV - 1)
+                + ROWS_DEV * (core - own_row)
+            )
+            distance = offset.astype(F32)
+            folded = distance - NY * jnp.round(distance * (1.0 / NY))
+            sine_d, cosine_d = small_sincos(folded * (math.pi / NY))
+            row_sign = (1 - 2 * (offset & 1)).astype(F32)
+            upper = (cosine_d * cosine_g + sine_d * sine_g) * row_sign
+            lower = sine_d * cosine_g - cosine_d * sine_g
+            turns = (distance - nearest) * (1.0 / NY)
+            at_peak = turns == jnp.round(turns)
+            lower = jnp.where(at_peak, 1.0, lower)
+            shift_base[...] = jnp.where(at_peak, peak, -lobes * upper / lower)
+            for place in range(GRID_XH * GRID_Y):
+                for quad in range(GRID_Z // 4):
+                    tiles = []
+                    for pair in range(2):
+                        start = (quad * 4 + pair * 2) * 64 + place * 8
+                        tiles.append(
+                            (shift_base[start : start + 8, :], shift_base[start + 64 : start + 72, :])
+                        )
+                    target = half * (NY // 2) + place * 32 + quad * 16
+                    for row in range(ROWS_DEV):
+                        column = block * GROUP + row * PIX_BLK
+                        merged = []
+                        for left, right in tiles:
+                            if row < ROWS_DEV - 1:
+                                left = pltpu.roll(left, 5 + row, 0)
+                            merged.append(
+                                jnp.where(upper_rows, left, pltpu.roll(right, 1 + row, 0))
+                            )
+                        shift_ref[target : target + 16, column : column + PIX_BLK] = (
+                            jnp.concatenate(merged, axis=0).astype(BF16)
+                        )
 
     def transform(step, block):
         return jnp.dot(
@@ -246,78 +259,57 @@
                         top, only * middle_ref[which : which + 1, lanes], old
                     ).astype(BF16)
 
-    def multiply(step, rows):
-        products[step, rows, :] = lax.dot_general(
-            shift_ref[rows, :],
+    def multiply(step):
+        products[step] = lax.dot_general(
+            shift_ref[...],
             rotated[step],
             (((1,), (1,)), ((), ())),
             preferred_element_type=F32,
         )
 
-    even = (lax.broadcasted_iota(jnp.int32, (8, 2 * CHUNK), 0) & 1) == 0
-    upper_rows = lax.broadcasted_iota(jnp.int32, (8, PIX_BLK), 0) < ROWS_DEV
-    first_core = jnp.full((8, PIX_BLK), own_core, jnp.int32) == 0
-    height = CHUNK // 16
-
-    def store(step, z_range):
+    even = (lax.broadcasted_iota(jnp.int32, (32, 2 * CHUNK), 0) & 1) == 0
+
+    def store(step):
         edge_herm = products[step, NY : NY + 1, : 2 * CHUNK]
         edge_anti = products[step, NY : NY + 1, 2 * CHUNK :]
         edges = (
             jnp.where(even, -edge_anti, edge_anti),
             jnp.where(even, edge_herm, -edge_herm),
         )
-        for z_at in z_range:
-            for x_high in range(GRID_XH):
-                for y_at in range(GRID_Y):
-                    start = z_at * 64 + x_high * 32 + y_at * 8
-                    for band in range(GRID_BAND):
-                        slots = slice(band * 2 * CHUNK, (band + 1) * 2 * CHUNK)
-                        whole = products[step, start : start + 8, slots] + edges[band]
-                        kept, sent = [], []
-                        for lane in range(0, 2 * CHUNK, 2 * PIX_BLK):
-                            left = whole[:, lane : lane + PIX_BLK]
-                            right = whole[:, lane + PIX_BLK : lane + 2 * PIX_BLK]
-                            low = jnp.where(upper_rows, left, pltpu.roll(right, ROWS_DEV, 0))
-                            high = jnp.where(upper_rows, pltpu.roll(left, ROWS_DEV, 0), right)
-                            kept.append(jnp.where(first_core, low, high))
-                            sent.append(jnp.where(first_core, high, low))
-                        piece = (x_high * GRID_Y + y_at) * GRID_BAND + band
-                        target = z_at * 32 + step * height
-                        where = slice(target, target + height)
-                        keep_ref[piece, where, :] = jnp.concatenate(kept, axis=0)
-                        send_ref[piece, where, :] = jnp.concatenate(sent, axis=0).astype(BF16)
+        for half, out_ref in enumerate((keep_ref, send_ref)):
+            for place in range(GRID_XH * GRID_Y):
+                start = half * (NY // 2) + place * 32
+                for band in range(GRID_BAND):
+                    slots = slice(band * 2 * CHUNK, (band + 1) * 2 * CHUNK)
+                    whole = (products[step, start : start + 32, slots] + edges[band]).astype(
+                        out_ref.dtype
+                    )
+                    for tile in range(2 * CHUNK // PIX_BLK):
+                        target = (step * (2 * CHUNK // PIX_BLK) + tile) * 32
+                        out_ref[place * GRID_BAND + band, target : target + 32, :] = whole[
+                            :, tile * PIX_BLK : (tile + 1) * PIX_BLK
+                        ]
 
     def wait_for(copies):
         for copy in copies:
             copy.wait()
 
+    make_masks()
+    for block in range(BLK_BAND):
+        shift_block(block)
     wait_for(table_copies[:1] + block_copies[0])
-    spectrum = transform(0, 0)
-    make_masks()
-    rotate(0, 0, spectrum)
+    rotate(0, 0, transform(0, 0))
     wait_for(block_copies[1])
-    spectrum = transform(0, 1)
-    shift_block(0)
-    rotate(0, 1, spectrum)
+    rotate(0, 1, transform(0, 1))
     wait_for(block_copies[2] + table_copies[1:])
-    spectrum = transform(0, 2)
-    shift_block(1)
-    rotate(0, 2, spectrum)
-    spectrum = transform(1, 0)
-    shift_block(2)
-    rotate(1, 0, spectrum)
-    spectrum = transform(1, 1)
-    rotate(1, 1, spectrum)
-    spectrum = transform(1, 2)
-    multiply(0, slice(NY // 2, TALL))
-    rotate(1, 2, spectrum)
-    multiply(0, slice(0, NY // 2))
-    store(0, range(GRID_Z // 2, GRID_Z))
-    multiply(1, slice(NY // 2, TALL))
-    store(0, range(GRID_Z // 2))
-    multiply(1, slice(0, NY // 2))
-    store(1, range(GRID_Z // 2, GRID_Z))
-    store(1, range(GRID_Z // 2))
+    rotate(0, 2, transform(0, 2))
+    multiply(0)
+    rotate(1, 0, transform(1, 0))
+    rotate(1, 1, transform(1, 1))
+    store(0)
+    rotate(1, 2, transform(1, 2))
+    multiply(1)
+    store(1)
 
 
 VMEM_SPEC = pl.BlockSpec(memory_space=pltpu.VMEM)
@@ -325,20 +317,17 @@
 LOCAL_VMEM = 50 * 1024 * 1024
 
 
-def local_part(lists, counts, gradient, table, intens):
+def local_part(facts, table, intens):
     shape = (PIECES, 32 * GRID_Z, PIX_BLK)
     return pl.pallas_call(
         local_kernel,
-        in_specs=[HBM_SPEC] * 5,
+        in_specs=[VMEM_SPEC, HBM_SPEC, HBM_SPEC],
         out_specs=[VMEM_SPEC] * 2,
         out_shape=[jax.ShapeDtypeStruct(shape, F32), jax.ShapeDtypeStruct(shape, BF16)],
         scratch_shapes=[
-            pltpu.VMEM((CAP, NX), jnp.int32),
-            pltpu.VMEM((1, NX), jnp.int32),
-            pltpu.VMEM((2, PIX_BAND), F32),
             pltpu.VMEM((NX, DEPTH), BF16),
             pltpu.VMEM((NX, NX), BF16),
-            pltpu.VMEM((TALL, PIX_BAND), F32),
+            pltpu.VMEM((NY, PIX_BLK), F32),
             pltpu.VMEM((TALL, DEPTH), BF16),
             pltpu.VMEM((2, HALF_X // 8, PIX_BAND), F32),
             pltpu.VMEM((2, 8, PIX_BAND), F32),
@@ -347,17 +336,22 @@
             pltpu.VMEM((8, PIX_BLK), F32),
             pltpu.VMEM((STEPS, 4 * CHUNK, DEPTH), BF16),
             pltpu.VMEM((STEPS, TALL, 4 * CHUNK), F32),
-            pltpu.SemaphoreType.DMA((3 + STEPS + BLK_BAND * ROWS_DEV,)),
+            pltpu.SemaphoreType.DMA((STEPS + BLK_BAND * ROWS_DEV,)),
         ],
         compiler_params=pltpu.CompilerParams(vmem_limit_bytes=LOCAL_VMEM),
-    )(lists, counts, gradient, table, intens)
+    )(facts, table, intens)
 
 
 def plane_kernel(pieces_ref, plane_ref):
     total = pieces_ref[0].astype(F32)
     for source in range(1, PIECES):
         total = total + pieces_ref[source].astype(F32)
-    plane_ref[...] = total.astype(BF16)
+    for z_at in range(GRID_Z):
+        rows = [
+            total[tile * 32 + z_at * ROWS_DEV : tile * 32 + (z_at + 1) * ROWS_DEV]
+            for tile in range(NX // PIX_BLK)
+        ]
+        plane_ref[z_at] = jnp.concatenate(rows, axis=0).astype(BF16)
 
 
 def plane_part(pieces):
@@ -365,7 +359,7 @@
         plane_kernel,
         in_specs=[VMEM_SPEC],
         out_specs=VMEM_SPEC,
-        out_shape=jax.ShapeDtypeStruct((32 * GRID_Z, PIX_BLK), BF16),
+        out_shape=jax.ShapeDtypeStruct((GRID_Z, 32, PIX_BLK), BF16),
         compiler_params=pltpu.CompilerParams(vmem_limit_bytes=32 * 1024 * 1024),
     )(pieces)
 
@@ -395,15 +389,21 @@
 
 
 def body(intens, block_list, block_count, pixel_gradient):
-    keep, send = local_part(
-        block_list.T, block_count.T, pixel_gradient, jnp.asarray(forward_table()), intens
-    )
+    packed = block_list[:, 0] + 4 * block_list[:, 1] + 16 * block_count[:, 0]
+    facts = jnp.concatenate(
+        [
+            packed.astype(F32)[None],
+            jnp.pad(pixel_gradient, ((0, 5), (0, NX - PIX_BAND))),
+        ],
+        axis=0,
+    )
+    keep, send = local_part(facts, jnp.asarray(forward_table()), intens)
     received = lax.ppermute(send, "core", [(0, 1), (1, 0)])
     chip = (keep + received.astype(F32)).astype(BF16)
     pieces = lax.all_to_all(
         chip, ("xh", "y", "band"), split_axis=0, concat_axis=0, tiled=True
     )
-    plane = plane_part(pieces).reshape(GRID_Z, 32, PIX_BLK)
+    plane = plane_part(pieces)
     parts = lax.all_to_all(plane, "z", split_axis=0, concat_axis=0, tiled=True)
     return final_part(parts, jnp.asarray(backward_table()))
 

time: 59 us -> 57.7 us (0.978)
  local copies, waits for them, and re-layouts: 2.07 us -> 0.01 us
  other arithmetic: 0.3 us -> 1.78 us
  Pallas kernels: 13.3 us -> 12.6 us
    unnamed x8 -> x2, local copies, waits for them, and re-layouts: 2.07 us -> 0.01 us
    convert_element_type x0 -> x1, other arithmetic: none -> 0.78 us  [body(): packed.astype(F32)[None]]
    concatenate x0 -> x1, other arithmetic: none -> 0.7 us  [body(): jnp.concatenate([packed.astype(F32)[None], jnp.pad(pixel_gradient, ((0, 5...]
    pallas_call x1, Pallas kernels: 11.9 us -> 11.2 us  [local_part(): pl.pallas_call(local_kernel, in_specs=[VMEM_SPEC, HBM_SPEC, HBM_SPEC], ou...]
where the time goes in v5:
time: 57.7 us; the launch traced here: 57.5 us
  blocking collectives  40.3 us (70%)
  Pallas kernels  12.6 us (22%)
  waiting for transfers between devices  2.65 us (5%)
  other arithmetic  1.78 us (3%)
    all_to_all x1, blocking collectives, body(): lax.all_to_all(chip, ('xh', 'y', 'band'), split_axis=0, concat_axis=0, ti...  23.6 us
    all_to_all x1, blocking collectives, body(): parts = lax.all_to_all(plane, 'z', split_axis=0, concat_axis=0, tiled=True)  16.6 us
    pallas_call x1, Pallas kernels, local_part(): pl.pallas_call(local_kernel, in_specs=[VMEM_SPEC, HBM_SPEC, HBM_SPEC], ou...  11.2 us
    ppermute x1, waiting for transfers between devices, body(): received = lax.ppermute(send, 'core', [(0, 1), (1, 0)])  2.65 us
    pallas_call x1, Pallas kernels, final_part(): pl.pallas_call(final_kernel, in_specs=[VMEM_SPEC] * 2, out_specs=VMEM_SPE...  1.27 us
  transfers between devices with their start and end apart: 1, of which 1 were waited for; matrix products, arithmetic and copies ran while one was open for 0% of the time, Pallas kernels for 0%

profile of v5, /device:TPU:2, one launch (start us, length us, event | category | flops | bytes accessed | tf_op | source)
XLA Modules:
  0.0 57.5 jit_solution(5686520014515777718)
XLA Ops:
  0.0 0.8 %convert_bitcast_fusion = f32[1,1024]{1,0:T(1,128)S(1)} fusion(s32[1024,1]{0,1:T(1,128)} %param.8, s32[1024,2]{0,1:T(2,128)} %param.7), kind=kLoop, calls=%fused_computation.3 | loop fusion | flops 5120 | bytes 16384 | tf_op jit(solution)/shard_map/convert_element_type | solution.py:395
  0.8 0.7 %select_maximum_fusion.facts_ref = f32[8,1024]{1,0:T(8,128)S(1)} fusion(f32[2,384]{1,0:T(2,128)} %param.9, f32[1,1024]{1,0:T(1,128)S(1)} %convert_bitcast_fusion), kind=kLoop, calls=%fused_computation.1 | loop fusion | flops 24576 | bytes 39936 | tf_op jit(solution)/shard_map/concatenate | solution.py:393
  1.5 11.2 %shard_map.64 = (f32[16,256,128]{2,1,0:T(8,128)S(1)}, bf16[16,256,128]{2,1,0:T(8,128)(2,1)S(1)}) custom-call(f32[8,1024]{1,0:T(8,128)S(1)} %select_maximum_fusion.facts_ref, bf16[1024,1024]{1,0:T(8,128)(2,1)} %constant.11.clone.table_hbm, bf16[4,1024,384]{2,1,0:T(8,128)(2,1)} %intens_hbm.1), custom_call_target="tpu_custom_call" | custom-call | tf_op jit(solution)/shard_map/pallas_call | solution.py:322
  12.7 0.1 collective-permute-start
  12.8 2.6 %collective-permute-done = bf16[16,256,128]{2,1,0:T(8,128)(2,1)S(1)} collective-permute-done((bf16[16,256,128]{2,1,0:T(8,128)(2,1)S(1)}, bf16[16,256,128]{2,1,0:T(8,128)(2,1)S(1)}, u32[]{:S(2)}, u32[]{:S(2)}) %collective-permute-start) | collective-permute-done | bytes 1048608 | tf_op jit(solution)/shard_map/ppermute | solution.py:401
  15.5 0.0 copy-start
  15.5 0.3 add_convert_fusion
  15.8 23.6 %all_to_all.10.pieces_ref = bf16[16,256,128]{2,1,0:T(8,128)(2,1)S(1)} all-to-all(bf16[16,256,128]{2,1,0:T(8,128)(2,1)S(1)} %add_convert_fusion), channel_id=1, replica_groups=mesh['z'=8,'xh'=2,'y'=4,'core'=2,'band'=2] {'xh','y','band'}, dimensions={0} | all-to-all | bytes 2097152 | tf_op jit(solution)/shard_map/all_to_all | solution.py:403
  39.4 0.1 shard_map.65
  39.5 16.6 %all_to_all.11.parts_ref = bf16[8,32,128]{2,1,0:T(8,128)(2,1)S(1)} all-to-all(bf16[8,32,128]{2,1,0:T(8,128)(2,1)S(1)} %shard_map.65), channel_id=1, replica_groups=mesh['z'=8,'xh'=2,'y'=4,'core'=2,'band'=2] {'z'}, dimensions={0} | all-to-all | bytes 131072 | tf_op jit(solution)/shard_map/all_to_all | solution.py:407
  56.2 0.0 copy-done
  56.2 1.3 %shard_map.66 = f32[1,4,1024]{2,1,0:T(4,128)} custom-call(bf16[8,32,128]{2,1,0:T(8,128)(2,1)S(1)} %all_to_all.11.parts_ref, bf16[2,1024,1024]{2,1,0:T(8,128)(2,1)S(1)} %copy-done), custom_call_target="tpu_custom_call" | custom-call | tf_op jit(solution)/shard_map/pallas_call | solution.py:382
Async XLA Ops:
  12.7 2.7 %collective-permute-start = (bf16[16,256,128]{2,1,0:T(8,128)(2,1)S(1)}, bf16[16,256,128]{2,1,0:T(8,128)(2,1)S(1)}, u32[]{:S(2)}, u32[]{:S(2)}) collective-permute-start(bf16[16,256,128]{2,1,0:T(8,128)(2,1)S(1)} %get-tuple-element.8), channel_id=1, source_target_pairs={{0,2},{2,0},{1,3},{3,1},{4,6},{6,4},{5,7},{7,5},{8,10},{10,8},{9,1... | collective-permute-start | bytes 3145736 | tf_op jit(solution)/shard_map/ppermute | solution.py:401
  15.5 40.7 %copy-start = (bf16[2,1024,1024]{2,1,0:T(8,128)(2,1)S(1)}, bf16[2,1024,1024]{2,1,0:T(8,128)(2,1)}, u32[]{:S(2)}) copy-start(bf16[2,1024,1024]{2,1,0:T(8,128)(2,1)} %constant.12.clone.table_ref) | copy-start | bytes 12582916

commit v6 on v5

--- a/solution.py
+++ b/solution.py
@@ -29,31 +29,30 @@
 F32, BF16 = jnp.float32, jnp.bfloat16
 
 
+def table_angles():
+    freqs = np.concatenate([np.arange(0, HALF_X, 2), np.arange(1, HALF_X, 2)])
+    return (np.outer(freqs, np.arange(HALF_X)) % NX) * (2.0 * math.pi / NX)
+
+
+def stack_parts(upper, lower):
+    pieces = [part.reshape(STEPS, CHUNK, HALF_X) for part in (upper, lower)]
+    return np.stack(pieces, axis=1).reshape(NX, HALF_X)
+
+
 def forward_table():
-    turns = np.outer(np.arange(HALF_X + 1), np.arange(NX)) % NX
-    angle = turns.astype(np.float32) * np.float32(2.0 * math.pi / NX)
-    norm_factor = np.float32(1.0 / math.sqrt(NX))
-    cosine, sine = np.cos(angle) * norm_factor, np.sin(angle) * norm_factor
-    lower = -sine[:HALF_X]
-    lower[0] = cosine[HALF_X]
-    pieces = np.stack(
-        [cosine[:HALF_X].reshape(STEPS, CHUNK, NX), lower.reshape(STEPS, CHUNK, NX)], axis=1
-    )
-    return pieces.reshape(NX, NX).astype(ml_dtypes.bfloat16)
+    angle = table_angles()
+    upper, lower = np.cos(angle), -np.sin(angle)
+    lower[0] = (-1.0) ** np.arange(HALF_X)
+    return (stack_parts(upper, lower) / math.sqrt(NX)).astype(ml_dtypes.bfloat16)
 
 
 def backward_table():
-    turns = np.outer(np.arange(HALF_X + 1), np.arange(NX)) % NX
-    angle = turns.astype(np.float64) * (2.0 * math.pi / NX)
+    angle = table_angles()
+    upper, lower = np.cos(angle), -np.sin(angle)
+    upper[0] *= 0.5
+    lower[0] = (-1.0) ** np.arange(HALF_X)
     scale = 1.0 / math.sqrt(NX) / math.sqrt(GRID_BAND * CAP * PIX_BLK)
-    upper = np.cos(angle[:HALF_X]) * scale
-    upper[0] *= 0.5
-    lower = -np.sin(angle[:HALF_X]) * scale
-    lower[0] = np.cos(angle[HALF_X]) * scale
-    pieces = np.stack(
-        [upper.reshape(STEPS, CHUNK, NX), lower.reshape(STEPS, CHUNK, NX)], axis=1
-    )
-    whole = pieces.reshape(NX, NX).astype(np.float32)
+    whole = (stack_parts(upper, lower) * scale).astype(np.float32)
     high = whole.astype(ml_dtypes.bfloat16)
     low = (whole - high.astype(np.float32)).astype(ml_dtypes.bfloat16)
     return np.stack([high, low])
@@ -93,12 +92,15 @@
     keep_ref,
     send_ref,
     values,
+    folded,
     table_ref,
     shift_base,
     shift_ref,
     coarse_ref,
     fine_ref,
     middle_ref,
+    row_facts,
+    columns_ref,
     masks_ref,
     middle_used,
     rotated,
@@ -128,10 +130,13 @@
 
     gradient_x = facts_ref[1:2, 0:PIX_BAND]
     gradient_y = facts_ref[2:3, 0:PIX_BAND]
-    eights = lax.broadcasted_iota(jnp.int32, (HALF_X // 8, PIX_BAND), 0).astype(F32)
-    coarse_ref[0], coarse_ref[1] = cycles_sincos(gradient_x * (eights * (8.0 / NX)))
-    units = lax.broadcasted_iota(jnp.int32, (8, PIX_BAND), 0).astype(F32)
-    fine_ref[0], fine_ref[1] = cycles_sincos(gradient_x * (units * (1.0 / NX)))
+    octets = lax.broadcasted_iota(jnp.int32, (CHUNK // 8, PIX_BAND), 0).astype(F32)
+    coarse_ref[0], coarse_ref[1] = cycles_sincos(gradient_x * (octets * (16.0 / NX)))
+    units = lax.broadcasted_iota(jnp.int32, (8, PIX_BAND), 0).astype(F32) * 2.0
+    for step in range(STEPS):
+        fine_ref[step, 0], fine_ref[step, 1] = cycles_sincos(
+            gradient_x * ((units + step) * (1.0 / NX))
+        )
     middle_ref[0:1, :], middle_ref[1:2, :] = cycles_sincos(gradient_x * 0.5)
 
     def make_masks():
@@ -153,14 +158,30 @@
         ahead = used[:, :HALF_X]
         mirror = jnp.where(lane_first, ahead, mirror)
         for sort, rows in enumerate((ahead + mirror, ahead - mirror)):
-            columns = rows.T
-            for block in range(BLK_BAND):
-                masks_ref[sort * BLK_BAND + block] = jnp.broadcast_to(
-                    columns[:, block : block + 1], (HALF_X, PIX_BLK)
-                ).astype(BF16)
+            columns_ref[sort] = rows.T
+            for step in range(STEPS):
+                columns = columns_ref[sort, pl.ds(step, CHUNK, stride=2), :]
+                for block in range(BLK_BAND):
+                    masks_ref[
+                        sort * BLK_BAND + block, step * CHUNK : (step + 1) * CHUNK
+                    ] = jnp.broadcast_to(
+                        columns[:, block : block + 1], (CHUNK, PIX_BLK)
+                    ).astype(BF16)
         middle_used[...] = jnp.broadcast_to(used[:, HALF_X : HALF_X + 1], (8, PIX_BLK))
 
     upper_rows = lax.broadcasted_iota(jnp.int32, (8, PIX_BLK), 0) < ROWS_DEV
+    for half in range(GRID_CORE):
+        core = own_core if half == 0 else 1 - own_core
+        offset = (
+            lax.broadcasted_iota(jnp.int32, (NY, PIX_BLK), 0)
+            - (ROWS_DEV - 1)
+            + ROWS_DEV * (core - own_row)
+        )
+        distance = offset.astype(F32)
+        folded_distance = distance - NY * jnp.round(distance * (1.0 / NY))
+        row_facts[half, 0] = distance
+        row_facts[half, 1], row_facts[half, 2] = small_sincos(folded_distance * (math.pi / NY))
+        row_facts[half, 3] = (1 - 2 * (offset & 1)).astype(F32)
 
     def shift_block(block):
         lanes = slice(block * PIX_BLK, (block + 1) * PIX_BLK)
@@ -180,16 +201,8 @@
                 first_row, lobes * (1.0 - 2.0 * (row % 2)), 0.0
             ).astype(BF16)
         for half in range(GRID_CORE):
-            core = own_core if half == 0 else 1 - own_core
-            offset = (
-                lax.broadcasted_iota(jnp.int32, (NY, PIX_BLK), 0)
-                - (ROWS_DEV - 1)
-                + ROWS_DEV * (core - own_row)
-            )
-            distance = offset.astype(F32)
-            folded = distance - NY * jnp.round(distance * (1.0 / NY))
-            sine_d, cosine_d = small_sincos(folded * (math.pi / NY))
-            row_sign = (1 - 2 * (offset & 1)).astype(F32)
+            distance, sine_d, cosine_d = (row_facts[half, which] for which in range(3))
+            row_sign = row_facts[half, 3]
             upper = (cosine_d * cosine_g + sine_d * sine_g) * row_sign
             lower = sine_d * cosine_g - cosine_d * sine_g
             turns = (distance - nearest) * (1.0 / NY)
@@ -218,19 +231,25 @@
                             jnp.concatenate(merged, axis=0).astype(BF16)
                         )
 
+    def fold(block):
+        columns = slice(block * GROUP, (block + 1) * GROUP)
+        near, far = values[:HALF_X, columns], values[HALF_X:, columns]
+        folded[0, :, columns] = near + far
+        folded[1, :, columns] = near - far
+
     def transform(step, block):
         return jnp.dot(
             table_ref[step * 2 * CHUNK : (step + 1) * 2 * CHUNK, :],
-            values[:, block * GROUP : (block + 1) * GROUP],
+            folded[step, :, block * GROUP : (block + 1) * GROUP],
             preferred_element_type=F32,
         )
 
     def rotate(step, block, spectrum):
         lanes = slice(block * PIX_BLK, (block + 1) * PIX_BLK)
         spectrum = spectrum.astype(BF16).astype(F32)
-        fine_sine, fine_cosine = fine_ref[0, :, lanes], fine_ref[1, :, lanes]
+        fine_sine, fine_cosine = fine_ref[step, 0, :, lanes], fine_ref[step, 1, :, lanes]
         sines, cosines = [], []
-        for octet in range(step * CHUNK // 8, (step + 1) * CHUNK // 8):
+        for octet in range(CHUNK // 8):
             sine_c = coarse_ref[0, octet : octet + 1, lanes]
             cosine_c = coarse_ref[1, octet : octet + 1, lanes]
             sines.append(sine_c * fine_cosine + cosine_c * fine_sine)
@@ -298,10 +317,13 @@
     for block in range(BLK_BAND):
         shift_block(block)
     wait_for(table_copies[:1] + block_copies[0])
+    fold(0)
     rotate(0, 0, transform(0, 0))
     wait_for(block_copies[1])
+    fold(1)
     rotate(0, 1, transform(0, 1))
     wait_for(block_copies[2] + table_copies[1:])
+    fold(2)
     rotate(0, 2, transform(0, 2))
     multiply(0)
     rotate(1, 0, transform(1, 0))
@@ -326,12 +348,15 @@
         out_shape=[jax.ShapeDtypeStruct(shape, F32), jax.ShapeDtypeStruct(shape, BF16)],
         scratch_shapes=[
             pltpu.VMEM((NX, DEPTH), BF16),
-            pltpu.VMEM((NX, NX), BF16),
+            pltpu.VMEM((STEPS, HALF_X, DEPTH), BF16),
+            pltpu.VMEM((NX, HALF_X), BF16),
             pltpu.VMEM((NY, PIX_BLK), F32),
             pltpu.VMEM((TALL, DEPTH), BF16),
-            pltpu.VMEM((2, HALF_X // 8, PIX_BAND), F32),
-            pltpu.VMEM((2, 8, PIX_BAND), F32),
+            pltpu.VMEM((2, CHUNK // 8, PIX_BAND), F32),
+            pltpu.VMEM((STEPS, 2, 8, PIX_BAND), F32),
             pltpu.VMEM((2, PIX_BAND), F32),
+            pltpu.VMEM((GRID_CORE, 4, NY, PIX_BLK), F32),
+            pltpu.VMEM((2, HALF_X, 8), F32),
             pltpu.VMEM((2 * BLK_BAND, HALF_X, PIX_BLK), BF16),
             pltpu.VMEM((8, PIX_BLK), F32),
             pltpu.VMEM((STEPS, 4 * CHUNK, DEPTH), BF16),
@@ -373,9 +398,17 @@
     high = total.astype(BF16)
     low = total - high.astype(F32)
     both = jnp.concatenate([high.astype(F32), low], axis=0).astype(BF16)
-    image = jnp.dot(both, table_ref[0], preferred_element_type=F32)
-    image = image[:ROWS_DEV] + image[ROWS_DEV:]
-    image_ref[0] = image + jnp.dot(high, table_ref[1], preferred_element_type=F32)
+    halves = []
+    for step in range(STEPS):
+        slots = slice(step * 2 * CHUNK, (step + 1) * 2 * CHUNK)
+        image = jnp.dot(both[:, slots], table_ref[0, slots], preferred_element_type=F32)
+        image = image[:ROWS_DEV] + image[ROWS_DEV:]
+        halves.append(
+            image
+            + jnp.dot(high[:, slots], table_ref[1, slots], preferred_element_type=F32)
+        )
+    image_ref[0, :, :HALF_X] = halves[0] + halves[1]
+    image_ref[0, :, HALF_X:] = halves[0] - halves[1]
 
 
 def final_part(parts, table):

time: 57.7 us -> 59.9 us (1.038)
  other arithmetic: 1.78 us -> 3.37 us
  local copies, waits for them, and re-layouts: 0.01 us -> 1.23 us
    convert_element_type x1, other arithmetic: 0.3 us -> 1.89 us  [body(): chip = (keep + received.astype(F32)).astype(BF16)]
    unnamed x2 -> x4, local copies, waits for them, and re-layouts: 0.01 us -> 1.23 us
where the time goes in v6:
time: 59.9 us; the launch traced here: 59.6 us
  blocking collectives  40.1 us (67%)
  Pallas kernels  12.1 us (20%)
  other arithmetic  3.37 us (6%)
  waiting for transfers between devices  2.65 us (4%)
  local copies, waits for them, and re-layouts  1.23 us (2%)
    all_to_all x1, blocking collectives, body(): lax.all_to_all(chip, ('xh', 'y', 'band'), split_axis=0, concat_axis=0, ti...  23.5 us
    all_to_all x1, blocking collectives, body(): parts = lax.all_to_all(plane, 'z', split_axis=0, concat_axis=0, tiled=True)  16.6 us
    pallas_call x1, Pallas kernels, local_part(): pl.pallas_call(local_kernel, in_specs=[VMEM_SPEC, HBM_SPEC, HBM_SPEC], ou...  11 us
    ppermute x1, waiting for transfers between devices, body(): received = lax.ppermute(send, 'core', [(0, 1), (1, 0)])  2.65 us
    convert_element_type x1, other arithmetic, body(): chip = (keep + received.astype(F32)).astype(BF16)  1.89 us
    unnamed x4, local copies, waits for them, and re-layouts  1.23 us
  transfers between devices with their start and end apart: 1, of which 1 were waited for; matrix products, arithmetic and copies ran while one was open for 0% of the time, Pallas kernels for 0%

profile of v6, /device:TPU:2, one launch (start us, length us, event | category | flops | bytes accessed | tf_op | source)
XLA Modules:
  0.0 59.6 jit_solution(3362898999074907074)
XLA Ops:
  0.0 0.8 %convert_bitcast_fusion = f32[1,1024]{1,0:T(1,128)S(1)} fusion(s32[1024,1]{0,1:T(1,128)} %param.8, s32[1024,2]{0,1:T(2,128)} %param.7), kind=kLoop, calls=%fused_computation.3 | loop fusion | flops 5120 | bytes 16384 | tf_op jit(solution)/shard_map/convert_element_type | solution.py:428
  0.8 0.7 %select_maximum_fusion.facts_ref = f32[8,1024]{1,0:T(8,128)S(1)} fusion(f32[2,384]{1,0:T(2,128)} %param.9, f32[1,1024]{1,0:T(1,128)S(1)} %convert_bitcast_fusion), kind=kLoop, calls=%fused_computation.1 | loop fusion | flops 24576 | bytes 39936 | tf_op jit(solution)/shard_map/concatenate | solution.py:426
  1.5 0.0 copy-start.1
  1.5 1.2 %copy-done.1 = bf16[1024,512]{1,0:T(8,128)(2,1)S(1)} copy-done((bf16[1024,512]{1,0:T(8,128)(2,1)S(1)}, bf16[1024,512]{1,0:T(8,128)(2,1)}, u32[]{:S(2)}) %copy-start.1) | copy-done | bytes 1048600
  2.7 11.0 %shard_map.64 = (f32[16,256,128]{2,1,0:T(8,128)}, bf16[16,256,128]{2,1,0:T(8,128)(2,1)S(1)}) custom-call(f32[8,1024]{1,0:T(8,128)S(1)} %select_maximum_fusion.facts_ref, bf16[1024,512]{1,0:T(8,128)(2,1)S(1)} %copy-done.1, bf16[4,1024,384]{2,1,0:T(8,128)(2,1)} %intens_hbm.1), custom_call_target="tpu_custom_call" | custom-call | tf_op jit(solution)/shard_map/pallas_call | solution.py:344
  13.7 0.1 collective-permute-start
  13.8 2.6 %collective-permute-done = bf16[16,256,128]{2,1,0:T(8,128)(2,1)S(1)} collective-permute-done((bf16[16,256,128]{2,1,0:T(8,128)(2,1)S(1)}, bf16[16,256,128]{2,1,0:T(8,128)(2,1)S(1)}, u32[]{:S(2)}, u32[]{:S(2)}) %collective-permute-start) | collective-permute-done | bytes 1048608 | tf_op jit(solution)/shard_map/ppermute | solution.py:434
  16.4 1.9 %add_convert_fusion = bf16[16,256,128]{2,1,0:T(8,128)(2,1)S(1)} fusion(f32[16,256,128]{2,1,0:T(8,128)} %get-tuple-element.7, bf16[16,256,128]{2,1,0:T(8,128)(2,1)S(1)} %collective-permute-done), kind=kLoop, calls=%fused_computation | loop fusion | flops 1572864 | bytes 4194304 | tf_op jit(solution)/shard_map/convert_element_type | solution.py:435
  18.3 0.0 copy-start
  18.4 23.5 %all_to_all.10.pieces_ref = bf16[16,256,128]{2,1,0:T(8,128)(2,1)S(1)} all-to-all(bf16[16,256,128]{2,1,0:T(8,128)(2,1)S(1)} %add_convert_fusion), channel_id=1, replica_groups=mesh['z'=8,'xh'=2,'y'=4,'core'=2,'band'=2] {'xh','y','band'}, dimensions={0} | all-to-all | bytes 2097152 | tf_op jit(solution)/shard_map/all_to_all | solution.py:436
  41.8 0.1 shard_map.65
  42.0 16.6 %all_to_all.11.parts_ref = bf16[8,32,128]{2,1,0:T(8,128)(2,1)S(1)} all-to-all(bf16[8,32,128]{2,1,0:T(8,128)(2,1)S(1)} %shard_map.65), channel_id=1, replica_groups=mesh['z'=8,'xh'=2,'y'=4,'core'=2,'band'=2] {'z'}, dimensions={0} | all-to-all | bytes 131072 | tf_op jit(solution)/shard_map/all_to_all | solution.py:440
  58.6 0.0 copy-done
  58.6 1.0 %shard_map.66 = f32[1,4,1024]{2,1,0:T(4,128)} custom-call(bf16[8,32,128]{2,1,0:T(8,128)(2,1)S(1)} %all_to_all.11.parts_ref, bf16[2,1024,512]{2,1,0:T(8,128)(2,1)S(1)} %copy-done), custom_call_target="tpu_custom_call" | custom-call | tf_op jit(solution)/shard_map/pallas_call | solution.py:415
Async XLA Ops:
  1.5 1.2 %copy-start.1 = (bf16[1024,512]{1,0:T(8,128)(2,1)S(1)}, bf16[1024,512]{1,0:T(8,128)(2,1)}, u32[]{:S(2)}) copy-start(bf16[1024,512]{1,0:T(8,128)(2,1)} %constant.11.clone.table_hbm) | copy-start | bytes 3145732
  13.7 2.7 %collective-permute-start = (bf16[16,256,128]{2,1,0:T(8,128)(2,1)S(1)}, bf16[16,256,128]{2,1,0:T(8,128)(2,1)S(1)}, u32[]{:S(2)}, u32[]{:S(2)}) collective-permute-start(bf16[16,256,128]{2,1,0:T(8,128)(2,1)S(1)} %get-tuple-element.8), channel_id=1, source_target_pairs={{0,2},{2,0},{1,3},{3,1},{4,6},{6,4},{5,7},{7,5},{8,10},{10,8},{9,1... | collective-permute-start | bytes 3145736 | tf_op jit(solution)/shard_map/ppermute | solution.py:434
  18.3 40.3 %copy-start = (bf16[2,1024,512]{2,1,0:T(8,128)(2,1)S(1)}, bf16[2,1024,512]{2,1,0:T(8,128)(2,1)}, u32[]{:S(2)}) copy-start(bf16[2,1024,512]{2,1,0:T(8,128)(2,1)} %constant.12.clone.table_ref) | copy-start | bytes 6291460

commit v7 on v5

--- a/solution.py
+++ b/solution.py
@@ -43,7 +43,7 @@
 
 
 def backward_table():
-    turns = np.outer(np.arange(HALF_X + 1), np.arange(NX)) % NX
+    turns = np.outer(np.arange(HALF_X + 1), np.arange(HALF_X)) % NX
     angle = turns.astype(np.float64) * (2.0 * math.pi / NX)
     scale = 1.0 / math.sqrt(NX) / math.sqrt(GRID_BAND * CAP * PIX_BLK)
     upper = np.cos(angle[:HALF_X]) * scale
@@ -51,9 +51,9 @@
     lower = -np.sin(angle[:HALF_X]) * scale
     lower[0] = np.cos(angle[HALF_X]) * scale
     pieces = np.stack(
-        [upper.reshape(STEPS, CHUNK, NX), lower.reshape(STEPS, CHUNK, NX)], axis=1
-    )
-    whole = pieces.reshape(NX, NX).astype(np.float32)
+        [upper.reshape(STEPS, CHUNK, HALF_X), lower.reshape(STEPS, CHUNK, HALF_X)], axis=1
+    )
+    whole = pieces.reshape(NX, HALF_X).astype(np.float32)
     high = whole.astype(ml_dtypes.bfloat16)
     low = (whole - high.astype(np.float32)).astype(ml_dtypes.bfloat16)
     return np.stack([high, low])
@@ -370,12 +370,20 @@
         total = total + parts_ref[source].astype(F32)
     tiles = [total[at : at + ROWS_DEV] for at in range(0, 32, ROWS_DEV)]
     total = jnp.concatenate(tiles, axis=1)
-    high = total.astype(BF16)
-    low = total - high.astype(F32)
-    both = jnp.concatenate([high.astype(F32), low], axis=0).astype(BF16)
-    image = jnp.dot(both, table_ref[0], preferred_element_type=F32)
-    image = image[:ROWS_DEV] + image[ROWS_DEV:]
-    image_ref[0] = image + jnp.dot(high, table_ref[1], preferred_element_type=F32)
+    high = total.astype(BF16).astype(F32)
+    low = total - high
+    odd_slot = (lax.broadcasted_iota(jnp.int32, (ROWS_DEV, NX), 1) & 1) == 1
+    high_even, high_odd = jnp.where(odd_slot, 0.0, high), jnp.where(odd_slot, high, 0.0)
+    low_even, low_odd = jnp.where(odd_slot, 0.0, low), jnp.where(odd_slot, low, 0.0)
+    rows = jnp.concatenate([high_even, high_odd, low_even, low_odd], axis=0).astype(BF16)
+    image = jnp.dot(rows, table_ref[0], preferred_element_type=F32)
+    image = image[: 2 * ROWS_DEV] + image[2 * ROWS_DEV :]
+    image = image + jnp.dot(
+        rows[: 2 * ROWS_DEV], table_ref[1], preferred_element_type=F32
+    )
+    even, odd = image[:ROWS_DEV], image[ROWS_DEV:]
+    image_ref[0, :, :HALF_X] = even + odd
+    image_ref[0, :, HALF_X:] = even - odd
 
 
 def final_part(parts, table):

time: 57.7 us -> 57.3 us (level)
  no operation moved by 1% of the time
where the time goes in v7:
time: 57.3 us; the launch traced here: 57.1 us
  blocking collectives  40.1 us (70%)
  Pallas kernels  12.4 us (22%)
  waiting for transfers between devices  2.65 us (5%)
  other arithmetic  1.78 us (3%)
    all_to_all x1, blocking collectives, body(): lax.all_to_all(chip, ('xh', 'y', 'band'), split_axis=0, concat_axis=0, ti...  23.5 us
    all_to_all x1, blocking collectives, body(): parts = lax.all_to_all(plane, 'z', split_axis=0, concat_axis=0, tiled=True)  16.6 us
    pallas_call x1, Pallas kernels, local_part(): pl.pallas_call(local_kernel, in_specs=[VMEM_SPEC, HBM_SPEC, HBM_SPEC], ou...  11.2 us
    ppermute x1, waiting for transfers between devices, body(): received = lax.ppermute(send, 'core', [(0, 1), (1, 0)])  2.65 us
  transfers between devices with their start and end apart: 1, of which 1 were waited for; matrix products, arithmetic and copies ran while one was open for 0% of the time, Pallas kernels for 0%

profile of v7, /device:TPU:2, one launch (start us, length us, event | category | flops | bytes accessed | tf_op | source)
XLA Modules:
  0.0 57.1 jit_solution(5389009255434899838)
XLA Ops:
  0.0 0.8 %convert_bitcast_fusion = f32[1,1024]{1,0:T(1,128)S(1)} fusion(s32[1024,1]{0,1:T(1,128)} %param.8, s32[1024,2]{0,1:T(2,128)} %param.7), kind=kLoop, calls=%fused_computation.3 | loop fusion | flops 5120 | bytes 16384 | tf_op jit(solution)/shard_map/convert_element_type | solution.py:403
  0.8 0.7 %select_maximum_fusion.facts_ref = f32[8,1024]{1,0:T(8,128)S(1)} fusion(f32[2,384]{1,0:T(2,128)} %param.9, f32[1,1024]{1,0:T(1,128)S(1)} %convert_bitcast_fusion), kind=kLoop, calls=%fused_computation.1 | loop fusion | flops 24576 | bytes 39936 | tf_op jit(solution)/shard_map/concatenate | solution.py:401
  1.5 11.2 %shard_map.64 = (f32[16,256,128]{2,1,0:T(8,128)S(1)}, bf16[16,256,128]{2,1,0:T(8,128)(2,1)S(1)}) custom-call(f32[8,1024]{1,0:T(8,128)S(1)} %select_maximum_fusion.facts_ref, bf16[1024,1024]{1,0:T(8,128)(2,1)} %constant.11.clone.table_hbm, bf16[4,1024,384]{2,1,0:T(8,128)(2,1)} %intens_hbm.1), custom_call_target="tpu_custom_call" | custom-call | tf_op jit(solution)/shard_map/pallas_call | solution.py:322
  12.7 0.1 collective-permute-start
  12.8 2.6 %collective-permute-done = bf16[16,256,128]{2,1,0:T(8,128)(2,1)S(1)} collective-permute-done((bf16[16,256,128]{2,1,0:T(8,128)(2,1)S(1)}, bf16[16,256,128]{2,1,0:T(8,128)(2,1)S(1)}, u32[]{:S(2)}, u32[]{:S(2)}) %collective-permute-start) | collective-permute-done | bytes 1048608 | tf_op jit(solution)/shard_map/ppermute | solution.py:409
  15.5 0.3 add_convert_fusion
  15.8 0.0 copy-start
  15.8 23.5 %all_to_all.10.pieces_ref = bf16[16,256,128]{2,1,0:T(8,128)(2,1)S(1)} all-to-all(bf16[16,256,128]{2,1,0:T(8,128)(2,1)S(1)} %add_convert_fusion), channel_id=1, replica_groups=mesh['z'=8,'xh'=2,'y'=4,'core'=2,'band'=2] {'xh','y','band'}, dimensions={0} | all-to-all | bytes 2097152 | tf_op jit(solution)/shard_map/all_to_all | solution.py:411
  39.3 0.1 shard_map.65
  39.4 16.6 %all_to_all.11.parts_ref = bf16[8,32,128]{2,1,0:T(8,128)(2,1)S(1)} all-to-all(bf16[8,32,128]{2,1,0:T(8,128)(2,1)S(1)} %shard_map.65), channel_id=1, replica_groups=mesh['z'=8,'xh'=2,'y'=4,'core'=2,'band'=2] {'z'}, dimensions={0} | all-to-all | bytes 131072 | tf_op jit(solution)/shard_map/all_to_all | solution.py:415
  56.1 0.0 copy-done
  56.1 1.0 %shard_map.66 = f32[1,4,1024]{2,1,0:T(4,128)} custom-call(bf16[8,32,128]{2,1,0:T(8,128)(2,1)S(1)} %all_to_all.11.parts_ref, bf16[2,1024,512]{2,1,0:T(8,128)(2,1)S(1)} %copy-done), custom_call_target="tpu_custom_call" | custom-call | tf_op jit(solution)/shard_map/pallas_call | solution.py:390
Async XLA Ops:
  12.7 2.7 %collective-permute-start = (bf16[16,256,128]{2,1,0:T(8,128)(2,1)S(1)}, bf16[16,256,128]{2,1,0:T(8,128)(2,1)S(1)}, u32[]{:S(2)}, u32[]{:S(2)}) collective-permute-start(bf16[16,256,128]{2,1,0:T(8,128)(2,1)S(1)} %get-tuple-element.8), channel_id=1, source_target_pairs={{0,2},{2,0},{1,3},{3,1},{4,6},{6,4},{5,7},{7,5},{8,10},{10,8},{9,1... | collective-permute-start | bytes 3145736 | tf_op jit(solution)/shard_map/ppermute | solution.py:409
  15.8 40.3 %copy-start = (bf16[2,1024,512]{2,1,0:T(8,128)(2,1)S(1)}, bf16[2,1024,512]{2,1,0:T(8,128)(2,1)}, u32[]{:S(2)}) copy-start(bf16[2,1024,512]{2,1,0:T(8,128)(2,1)} %constant.12.clone.table_ref) | copy-start | bytes 6291460

commit v8 on v7

--- a/solution.py
+++ b/solution.py
@@ -123,7 +123,7 @@
                     copy_sem.at[STEPS + block * ROWS_DEV + row],
                 )
             )
-    for copy in table_copies[:1] + sum(block_copies, []) + table_copies[1:]:
+    for copy in table_copies[:1] + block_copies[0]:
         copy.start()
 
     gradient_x = facts_ref[1:2, 0:PIX_BAND]
@@ -294,15 +294,18 @@
         for copy in copies:
             copy.wait()
 
+    for copy in block_copies[1] + block_copies[2] + table_copies[1:]:
+        copy.start()
     make_masks()
-    for block in range(BLK_BAND):
-        shift_block(block)
+    shift_block(0)
+    shift_block(1)
     wait_for(table_copies[:1] + block_copies[0])
     rotate(0, 0, transform(0, 0))
     wait_for(block_copies[1])
     rotate(0, 1, transform(0, 1))
     wait_for(block_copies[2] + table_copies[1:])
     rotate(0, 2, transform(0, 2))
+    shift_block(2)
     multiply(0)
     rotate(1, 0, transform(1, 0))
     rotate(1, 1, transform(1, 1))

time: 57.3 us -> 57.1 us (level)
  no operation moved by 1% of the time
where the time goes in v8:
time: 57.1 us; the launch traced here: 56.9 us
  blocking collectives  40.1 us (70%)
  Pallas kernels  12.1 us (21%)
  waiting for transfers between devices  2.65 us (5%)
  other arithmetic  1.78 us (3%)
    all_to_all x1, blocking collectives, body(): lax.all_to_all(chip, ('xh', 'y', 'band'), split_axis=0, concat_axis=0, ti...  23.5 us
    all_to_all x1, blocking collectives, body(): parts = lax.all_to_all(plane, 'z', split_axis=0, concat_axis=0, tiled=True)  16.7 us
    pallas_call x1, Pallas kernels, local_part(): pl.pallas_call(local_kernel, in_specs=[VMEM_SPEC, HBM_SPEC, HBM_SPEC], ou...  11 us
    ppermute x1, waiting for transfers between devices, body(): received = lax.ppermute(send, 'core', [(0, 1), (1, 0)])  2.65 us
  transfers between devices with their start and end apart: 1, of which 1 were waited for; matrix products, arithmetic and copies ran while one was open for 0% of the time, Pallas kernels for 0%

profile of v8, /device:TPU:2, one launch (start us, length us, event | category | flops | bytes accessed | tf_op | source)
XLA Modules:
  0.0 56.9 jit_solution(9229323840343162239)
XLA Ops:
  0.0 0.8 %convert_bitcast_fusion = f32[1,1024]{1,0:T(1,128)S(1)} fusion(s32[1024,1]{0,1:T(1,128)} %param.8, s32[1024,2]{0,1:T(2,128)} %param.7), kind=kLoop, calls=%fused_computation.3 | loop fusion | flops 5120 | bytes 16384 | tf_op jit(solution)/shard_map/convert_element_type | solution.py:406
  0.8 0.7 %select_maximum_fusion.facts_ref = f32[8,1024]{1,0:T(8,128)S(1)} fusion(f32[2,384]{1,0:T(2,128)} %param.9, f32[1,1024]{1,0:T(1,128)S(1)} %convert_bitcast_fusion), kind=kLoop, calls=%fused_computation.1 | loop fusion | flops 24576 | bytes 39936 | tf_op jit(solution)/shard_map/concatenate | solution.py:404
  1.5 11.0 %shard_map.64 = (f32[16,256,128]{2,1,0:T(8,128)S(1)}, bf16[16,256,128]{2,1,0:T(8,128)(2,1)S(1)}) custom-call(f32[8,1024]{1,0:T(8,128)S(1)} %select_maximum_fusion.facts_ref, bf16[1024,1024]{1,0:T(8,128)(2,1)} %constant.11.clone.table_hbm, bf16[4,1024,384]{2,1,0:T(8,128)(2,1)} %intens_hbm.1), custom_call_target="tpu_custom_call" | custom-call | tf_op jit(solution)/shard_map/pallas_call | solution.py:325
  12.5 0.1 collective-permute-start
  12.6 2.6 %collective-permute-done = bf16[16,256,128]{2,1,0:T(8,128)(2,1)S(1)} collective-permute-done((bf16[16,256,128]{2,1,0:T(8,128)(2,1)S(1)}, bf16[16,256,128]{2,1,0:T(8,128)(2,1)S(1)}, u32[]{:S(2)}, u32[]{:S(2)}) %collective-permute-start) | collective-permute-done | bytes 1048608 | tf_op jit(solution)/shard_map/ppermute | solution.py:412
  15.2 0.3 add_convert_fusion
  15.6 0.0 copy-start
  15.6 23.5 %all_to_all.10.pieces_ref = bf16[16,256,128]{2,1,0:T(8,128)(2,1)S(1)} all-to-all(bf16[16,256,128]{2,1,0:T(8,128)(2,1)S(1)} %add_convert_fusion), channel_id=1, replica_groups=mesh['z'=8,'xh'=2,'y'=4,'core'=2,'band'=2] {'xh','y','band'}, dimensions={0} | all-to-all | bytes 2097152 | tf_op jit(solution)/shard_map/all_to_all | solution.py:414
  39.1 0.1 shard_map.65
  39.2 16.7 %all_to_all.11.parts_ref = bf16[8,32,128]{2,1,0:T(8,128)(2,1)S(1)} all-to-all(bf16[8,32,128]{2,1,0:T(8,128)(2,1)S(1)} %shard_map.65), channel_id=1, replica_groups=mesh['z'=8,'xh'=2,'y'=4,'core'=2,'band'=2] {'z'}, dimensions={0} | all-to-all | bytes 131072 | tf_op jit(solution)/shard_map/all_to_all | solution.py:418
  55.9 0.0 copy-done
  55.9 1.0 %shard_map.66 = f32[1,4,1024]{2,1,0:T(4,128)} custom-call(bf16[8,32,128]{2,1,0:T(8,128)(2,1)S(1)} %all_to_all.11.parts_ref, bf16[2,1024,512]{2,1,0:T(8,128)(2,1)S(1)} %copy-done), custom_call_target="tpu_custom_call" | custom-call | tf_op jit(solution)/shard_map/pallas_call | solution.py:393
Async XLA Ops:
  12.5 2.7 %collective-permute-start = (bf16[16,256,128]{2,1,0:T(8,128)(2,1)S(1)}, bf16[16,256,128]{2,1,0:T(8,128)(2,1)S(1)}, u32[]{:S(2)}, u32[]{:S(2)}) collective-permute-start(bf16[16,256,128]{2,1,0:T(8,128)(2,1)S(1)} %get-tuple-element.8), channel_id=1, source_target_pairs={{0,2},{2,0},{1,3},{3,1},{4,6},{6,4},{5,7},{7,5},{8,10},{10,8},{9,1... | collective-permute-start | bytes 3145736 | tf_op jit(solution)/shard_map/ppermute | solution.py:412
  15.6 40.3 %copy-start = (bf16[2,1024,512]{2,1,0:T(8,128)(2,1)S(1)}, bf16[2,1024,512]{2,1,0:T(8,128)(2,1)}, u32[]{:S(2)}) copy-start(bf16[2,1024,512]{2,1,0:T(8,128)(2,1)} %constant.12.clone.table_ref) | copy-start | bytes 6291460
